TPU v7x, 32 devices: a whole 2x2x4 slice. The times are simulated.
32 devices in a mesh: copies: 2 (over y), leaf: 4 (over z), sub: 4 (over x, core).
Axes of the slice: x: 2, y: 2, z: 4, core: 2. Of those that a mesh axis runs over, the one named last changes fastest.
Arguments:
- vectors: bfloat16 [512, 16, 128], P(('copies', 'leaf', 'sub')), parts along dimension 0, may hold values from -6 to 6
- leaf_basis: bfloat16 [512, 64, 128], P(('copies', 'leaf', 'sub')), parts along dimension 0, may hold values from -0.5 to 0.5
- near_blocks: bfloat16 [512, 6, 128, 128], P(('copies', 'leaf', 'sub')), parts along dimension 0, may hold values from -0.21875 to 0.21875
- near_list: int32 [256, 6], P(('leaf', 'sub')), may hold values from 0 to 255, as said below
- near_mask: int32 [256, 6], P(('leaf', 'sub')), may hold values from 0 to 1, as said below
- transfer_low: bfloat16 [960, 64, 64], P(('copies', 'leaf', 'sub')), parts along dimension 0, may hold values from -0.625 to 0.625
- coupling_low: bfloat16 [992, 3, 64, 64], P(('copies', 'leaf', 'sub')), parts along dimension 0, may hold values from -0.21875 to 0.21875
- far_list: int32 [496, 3], P(('leaf', 'sub')), may hold values from 0 to 255, as said below
- far_mask: int32 [496, 3], P(('leaf', 'sub')), may hold values from 0 to 1, as said below
- transfer_top: bfloat16 [60, 64, 64], P('copies'), parts along dimension 0, may hold values from -0.625 to 0.625
- coupling_top: bfloat16 [28, 3, 64, 64], P('copies'), parts along dimension 0, may hold values from -0.21875 to 0.21875
Outputs:
- product: bfloat16 [512, 16, 128], P(('copies', 'leaf', 'sub')), parts along dimension 0
There are 2 independent parts, one for each index of `copies`. A program takes and returns all parts, laid end to end along the dimension named above; an argument that names none is the same for every part. Nothing has to cross between parts.
Inputs may be any that keep to these rules, and one draw needn't show every extreme that they name: `near_list`: slots 0, 1, 2 of row i hold i - 1, i, i + 1 where those leaves exist; slots 3 and up in use hold, first and in any order, those candidates of leaf i that far_list does not couple at level 0; unused slots hold i; on every device some leaf uses all 6 slots. `near_mask`: 1 where the slot of near_list is in use. `far_list`: the slots in use of box t come first and hold candidates of t in its level, in any order; at levels 1 and up every candidate of t is in use; at level 0 every candidate of a leaf is either in use here or in near_list, never both; unused slots hold t. `far_mask`: 1 where the slot of far_list is in use; on every device some leaf uses all 3 slots.
All inputs are finite; a program needn't handle non-finite values.
Results may differ from a plain program's by a relative error of at most 0.0004.
Values may be sent and summed in bfloat16 or wider, within the bound.
A program may use at most 128 MiB of HBM per device.

v0:
```python
import jax
import jax.numpy as jnp
from jax import lax
from jax.sharding import PartitionSpec as P


def from_behind(shard, axis, by):
    length = lax.axis_size(axis)
    pairs = [(i, i + by) for i in range(length) if 0 <= i + by < length]
    return lax.ppermute(shard, axis, pairs)


def from_partner(block, axis, bit):
    count = lax.axis_size(axis)
    route = []
    for low in range(count):
        high = low | 1 << bit
        if high != low and high < count:
            route += [(low, high), (high, low)]
    return lax.ppermute(block, axis, route)


def per_device(
    vectors,
    leaf_basis,
    near_blocks,
    near_list,
    near_mask,
    transfer_low,
    coupling_low,
    far_list,
    far_mask,
    transfer_top,
    coupling_top,
):
    highest_level = lax.Precision.HIGHEST
    tree_devs = lax.axis_size(("leaf", "sub"))
    device = lax.axis_index(("leaf", "sub"))
    leaves = vectors.shape[0]
    num_vectors = vectors.shape[1]
    basis_rank = leaf_basis.shape[1]
    low_levels = leaves.bit_length()
    top_levels = tree_devs.bit_length() - 1
    edge_leaves = 3
    coefficient = jnp.einsum(
        "ivp,irp->ivr", vectors, leaf_basis, preferred_element_type=jnp.float32
    )
    level_list = [coefficient]
    starts = [0]
    for height in range(1, low_levels):
        box_count = level_list[-1].shape[0]
        first_box = starts[-1]
        pair_list = level_list[-1].reshape(box_count // 2, 2, num_vectors, basis_rank)
        matrix_stack = (
            transfer_low[first_box : first_box + box_count]
            .astype(jnp.float32)
            .reshape(box_count // 2, 2, basis_rank, basis_rank)
        )
        level_list.append(
            jnp.einsum("juyz,juza->jya", pair_list, matrix_stack, precision=highest_level)
        )
        starts.append(first_box + box_count)
    rim_counts = [min(3, level_list[height].shape[0]) for height in range(low_levels - 1)]
    left_parts = [
        level_list[height][level_list[height].shape[0] - rim_counts[height] :]
        for height in range(low_levels - 1)
    ]
    right_parts = [level_list[height][: rim_counts[height]] for height in range(low_levels - 1)]
    near_left, near_right = [
        from_behind(rim_piece, ("leaf", "sub"), distance)
        for rim_piece, distance in (
            (vectors[leaves - edge_leaves :], 1),
            (vectors[:edge_leaves], -1),
        )
    ]
    coef_left = []
    coef_right = []
    for height in range(low_levels - 1):
        got_left, got_right = [
            from_behind(rim_piece, ("leaf", "sub"), distance)
            for rim_piece, distance in ((left_parts[height], 1), (right_parts[height], -1))
        ]
        coef_left.append(got_left)
        coef_right.append(got_right)
    beside_all = jnp.concatenate([near_left, vectors, near_right], 0)
    positions = near_list - (device * leaves - edge_leaves)
    sources = beside_all[positions] * near_mask[:, :, None, None].astype(vectors.dtype)
    near_terms = jnp.einsum(
        "ikvp,ikpq->ivq", sources, near_blocks, preferred_element_type=jnp.float32
    )
    far_terms = []
    for height in range(low_levels - 1):
        box_count = level_list[height].shape[0]
        first_box = starts[height]
        around_coef = jnp.concatenate(
            [coef_left[height], level_list[height], coef_right[height]], 0
        )
        partners = far_list[first_box : first_box + box_count]
        in_use = far_mask[first_box : first_box + box_count].astype(jnp.float32)
        spot_rows = partners - (device * box_count - rim_counts[height])
        gathered = around_coef[spot_rows] * in_use[:, :, None, None]
        matrix_stack = coupling_low[first_box : first_box + box_count].astype(jnp.float32)
        far_terms.append(
            jnp.einsum("tkvr,tkrs->tvs", gathered, matrix_stack, precision=highest_level)
        )
    offset_steps = (-3, -2, 2, 3)
    own_root = level_list[-1][0]
    fetched = []
    current_level = own_root
    for height in range(top_levels - 1):
        if height >= 1:
            sibling = from_partner(current_level, ("leaf", "sub"), height - 1)
            low_bit = device // (1 << height - 1) % 2
            left_coef = jnp.where(low_bit == 0, current_level, sibling)
            right_coef = jnp.where(low_bit == 0, sibling, current_level)
            node_index = device // (1 << height)
            first_box = 2 * tree_devs - 2 * (tree_devs >> height - 1)
            pair_mats = lax.dynamic_slice_in_dim(
                transfer_top, first_box + 2 * node_index, 2, 0
            ).astype(jnp.float32)
            current_level = jnp.dot(left_coef, pair_mats[0], precision=highest_level) + jnp.dot(
                right_coef, pair_mats[1], precision=highest_level
            )
        fetched.append(
            [
                from_behind(current_level, ("leaf", "sub"), -stride * (1 << height))
                for stride in offset_steps
            ]
        )
    root_row = starts[low_levels - 1]
    downward = jnp.zeros((num_vectors, basis_rank), jnp.float32)
    for height in range(top_levels - 2, -1, -1):
        node_index = device // (1 << height)
        own_mat = lax.dynamic_index_in_dim(
            transfer_top, 2 * tree_devs - 2 * (tree_devs >> height) + node_index, 0, keepdims=False
        ).astype(jnp.float32)
        nearby = fetched[height]
        stacked = jnp.stack(nearby, 0)
        if height == 0:
            top_partners = far_list[root_row]
            top_in_use = far_mask[root_row].astype(jnp.float32)
            relative = top_partners - device
            choose_slot = (relative[:, None] == jnp.array(offset_steps, jnp.int32)[None, :]).astype(
                jnp.float32
            ) * top_in_use[:, None]
            chosen = jnp.einsum("kj,jvr->kvr", choose_slot, stacked, precision=highest_level)
            top_matrix_stack = coupling_low[root_row].astype(jnp.float32)
        else:
            top_node_index = device // (1 << height)
            is_even = top_node_index % 2 == 0
            chosen = jnp.where(is_even, stacked[1:], stacked[:3])
            top_matrix_stack = lax.dynamic_index_in_dim(
                coupling_top,
                tree_devs - 2 * (tree_devs >> height) + top_node_index,
                0,
                keepdims=False,
            ).astype(jnp.float32)
        downward = jnp.einsum(
            "kvr,krs->vs", chosen, top_matrix_stack, precision=highest_level
        ) + jnp.dot(downward, own_mat.T, precision=highest_level)
    expanded = downward[None]
    for height in range(low_levels - 2, -1, -1):
        box_count = level_list[height].shape[0]
        matrix_stack = transfer_low[starts[height] : starts[height] + box_count].astype(jnp.float32)
        spread = jnp.repeat(expanded, 2, axis=0)
        expanded = far_terms[height] + jnp.einsum(
            "tvs,trs->tvr", spread, matrix_stack, precision=highest_level
        )
    leaf_term = jnp.einsum(
        "ivr,irp->ivp", expanded, leaf_basis.astype(jnp.float32), precision=highest_level
    )
    return (near_terms + leaf_term).astype(jnp.bfloat16)


def solution(mesh):
    in_specs = (
        P(("copies", "leaf", "sub"), None, None),
        P(("copies", "leaf", "sub"), None, None),
        P(("copies", "leaf", "sub"), None, None, None),
        P(("leaf", "sub"), None),
        P(("leaf", "sub"), None),
        P(("copies", "leaf", "sub"), None, None),
        P(("copies", "leaf", "sub"), None, None, None),
        P(("leaf", "sub"), None),
        P(("leaf", "sub"), None),
        P("copies", None, None),
        P("copies", None, None, None),
    )
    out_specs = P(("copies", "leaf", "sub"), None, None)
    return jax.shard_map(
        per_device, mesh=mesh, in_specs=in_specs, out_specs=out_specs, check_vma=False
    )
```

profile of v0, /device:TPU:1, one launch (start us, length us, event | category | flops | bytes accessed | tf_op | source)
XLA Modules:
  0.0 114.0 jit_solution(3228332580673249247)
XLA Ops:
  0.1 1.4 %fusion.91 = f32[16,16,64]{2,1,0:T(8,128)S(1)} fusion(bf16[16,16,128]{2,1,0:T(8,128)(2,1)} %param.12, bf16[16,64,128]{2,1,0:T(8,128)(2,1)} %param.13), kind=kOutput, calls=%fused_computation.144 | convolution fusion | flops 4194304 | bytes 393216 | tf_op jit(solution)/shard_map/ivp,irp->ivr/dot_general | solution.py:45
  3.4 4.5 %collective-permute-start.10 = (f32[16,64]{1,0:T(8,128)S(1)}, f32[16,64]{1,0:T(8,128)S(1)}, u32[]{:S(2)}, u32[]{:S(2)}) collective-permute-start(f32[16,64]{1,0:T(8,128)S(1)} %convolution_bitcast_fusion.9), channel_id=1, source_target_pairs={{0,3},{1,4},{2,5},{3,6},{4,7},{5,8},{6,9},{7,10},{8,11},{9,12},{10... | collective-permute-start | bytes 12296 | tf_op jit(solution)/shard_map/ppermute | solution.py:10
  7.9 3.3 %collective-permute-start.11 = (f32[16,64]{1,0:T(8,128)S(1)}, f32[16,64]{1,0:T(8,128)S(1)}, u32[]{:S(2)}, u32[]{:S(2)}) collective-permute-start(f32[16,64]{1,0:T(8,128)S(1)} %convolution_bitcast_fusion.9), channel_id=1, source_target_pairs={{0,2},{1,3},{2,4},{3,5},{4,6},{5,7},{6,8},{7,9},{8,10},{9,11},{10,... | collective-permute-start | bytes 12296 | tf_op jit(solution)/shard_map/ppermute | solution.py:10
  11.2 1.3 %collective-permute-start.12 = (f32[16,64]{1,0:T(8,128)S(1)}, f32[16,64]{1,0:T(8,128)S(1)}, u32[]{:S(2)}, u32[]{:S(2)}) collective-permute-start(f32[16,64]{1,0:T(8,128)S(1)} %convolution_bitcast_fusion.9), channel_id=1, source_target_pairs={{2,0},{3,1},{4,2},{5,3},{6,4},{7,5},{8,6},{9,7},{10,8},{11,9},{12,... | collective-permute-start | bytes 12296 | tf_op jit(solution)/shard_map/ppermute | solution.py:10
  12.5 1.3 %collective-permute-start.13 = (f32[16,64]{1,0:T(8,128)S(1)}, f32[16,64]{1,0:T(8,128)S(1)}, u32[]{:S(2)}, u32[]{:S(2)}) collective-permute-start(f32[16,64]{1,0:T(8,128)S(1)} %convolution_bitcast_fusion.9), channel_id=1, source_target_pairs={{3,0},{4,1},{5,2},{6,3},{7,4},{8,5},{9,6},{10,7},{11,8},{12,9},{13... | collective-permute-start | bytes 12296 | tf_op jit(solution)/shard_map/ppermute | solution.py:10
  14.2 1.4 %fusion.87 = (f32[3,16,64]{2,1,0:T(8,128)}, f32[3,16,64]{2,1,0:T(8,128)}) fusion(f32[16,16,64]{2,1,0:T(8,128)} %copy-done.3), kind=kLoop, calls=%fused_computation.140 | loop fusion | bytes 49152 | tf_op jit(solution)/shard_map/slice | solution.py:65
  15.6 1.3 %fusion.89 = (bf16[3,16,128]{2,1,0:T(8,128)(2,1)}, bf16[3,16,128]{2,1,0:T(8,128)(2,1)}) fusion(bf16[16,16,128]{2,1,0:T(8,128)(2,1)} %param.12), kind=kLoop, calls=%fused_computation.142 | loop fusion | bytes 49152 | tf_op jit(solution)/shard_map/slice | solution.py:72
  18.3 1.4 %fusion.88 = (f32[3,16,64]{2,1,0:T(8,128)}, f32[3,16,64]{2,1,0:T(8,128)}) fusion(f32[8,16,64]{2,1,0:T(8,128)} %bitcast.115), kind=kLoop, calls=%fused_computation.141 | loop fusion | bytes 49152 | tf_op jit(solution)/shard_map/slice | solution.py:65
  24.9 4.9 %collective-permute-start.8 = (f32[2,16,64]{2,1,0:T(8,128)S(1)}, f32[2,16,64]{2,1,0:T(8,128)S(1)}, u32[]{:S(2)}, u32[]{:S(2)}) collective-permute-start(f32[2,16,64]{2,1,0:T(8,128)S(1)} %convolution_bitcast_fusion.5), channel_id=1, source_target_pairs={{0,1},{1,2},{2,3},{3,4},{4,5},{5,6},{6,7},{7,8},{8,9},{9,10},{10,1... | collective-permute-start | bytes 24584 | tf_op jit(solution)/shard_map/ppermute | solution.py:10
  30.6 0.9 convolution_add_fusion.9
  31.4 1.9 %collective-permute-start.9 = (f32[2,16,64]{2,1,0:T(8,128)S(1)}, f32[2,16,64]{2,1,0:T(8,128)S(1)}, u32[]{:S(2)}, u32[]{:S(2)}) collective-permute-start(f32[2,16,64]{2,1,0:T(8,128)S(1)} %convolution_bitcast_fusion.5), channel_id=1, source_target_pairs={{1,0},{2,1},{3,2},{4,3},{5,4},{6,5},{7,6},{8,7},{9,8},{10,9},{11,1... | collective-permute-start | bytes 24584 | tf_op jit(solution)/shard_map/ppermute | solution.py:10
  33.4 2.8 %collective-permute-start.19 = (f32[16,64]{1,0:T(8,128)S(1)}, f32[16,64]{1,0:T(8,128)S(1)}, u32[]{:S(2)}, u32[]{:S(2)}) collective-permute-start(f32[16,64]{1,0:T(8,128)S(1)} %convolution_add_fusion.9), channel_id=1, source_target_pairs={{0,2},{2,0},{1,3},{3,1},{4,6},{6,4},{5,7},{7,5},{8,10},{10,8},{9,1... | collective-permute-start | bytes 12296 | tf_op jit(solution)/shard_map/ppermute | solution.py:20
  36.2 3.2 %collective-permute-start.15 = (f32[16,64]{1,0:T(8,128)S(1)}, f32[16,64]{1,0:T(8,128)S(1)}, u32[]{:S(2)}, u32[]{:S(2)}) collective-permute-start(f32[16,64]{1,0:T(8,128)S(1)} %convolution_add_fusion.9), channel_id=1, source_target_pairs={{0,4},{1,5},{2,6},{3,7},{4,8},{5,9},{6,10},{7,11},{8,12},{9,13},{1... | collective-permute-start | bytes 12296 | tf_op jit(solution)/shard_map/ppermute | solution.py:10
  39.4 1.3 %collective-permute-start.16 = (f32[16,64]{1,0:T(8,128)S(1)}, f32[16,64]{1,0:T(8,128)S(1)}, u32[]{:S(2)}, u32[]{:S(2)}) collective-permute-start(f32[16,64]{1,0:T(8,128)S(1)} %convolution_add_fusion.9), channel_id=1, source_target_pairs={{4,0},{5,1},{6,2},{7,3},{8,4},{9,5},{10,6},{11,7},{12,8},{13,9},{1... | collective-permute-start | bytes 12296 | tf_op jit(solution)/shard_map/ppermute | solution.py:10
  40.7 0.9 fusion.20
  41.6 1.0 convolution_bitcast_fusion.8
  42.7 1.3 %collective-permute-start.17 = (f32[16,64]{1,0:T(8,128)S(1)}, f32[16,64]{1,0:T(8,128)S(1)}, u32[]{:S(2)}, u32[]{:S(2)}) collective-permute-start(f32[16,64]{1,0:T(8,128)S(1)} %convolution_add_fusion.9), channel_id=1, source_target_pairs={{6,0},{7,1},{8,2},{9,3},{10,4},{11,5},{12,6},{13,7},{14,8},{15,9},... | collective-permute-start | bytes 12296 | tf_op jit(solution)/shard_map/ppermute | solution.py:10
  44.8 0.9 convolution_add_fusion.8
  45.7 5.5 %collective-permute-start.18 = (f32[16,64]{1,0:T(8,128)S(1)}, f32[16,64]{1,0:T(8,128)}, u32[]{:S(2)}, u32[]{:S(2)}) collective-permute-start(f32[16,64]{1,0:T(8,128)S(1)} %convolution_add_fusion.9), channel_id=1, source_target_pairs={{0,6},{1,7},{2,8},{3,9},{4,10},{5,11},{6,12},{7,13},{8,14},{9,15},... | collective-permute-start | bytes 12296 | tf_op jit(solution)/shard_map/ppermute | solution.py:10
  51.1 5.0 %collective-permute-start.20 = (f32[16,64]{1,0:T(8,128)S(1)}, f32[16,64]{1,0:T(8,128)}, u32[]{:S(2)}, u32[]{:S(2)}) collective-permute-start(f32[16,64]{1,0:T(8,128)S(1)} %convolution_add_fusion.8), channel_id=1, source_target_pairs={{0,8},{1,9},{2,10},{3,11},{4,12},{5,13},{6,14},{7,15},{16,24},{17,... | collective-permute-start | bytes 12296 | tf_op jit(solution)/shard_map/ppermute | solution.py:10
  56.7 1.3 %collective-permute-start.21 = (f32[16,64]{1,0:T(8,128)S(1)}, f32[16,64]{1,0:T(8,128)S(1)}, u32[]{:S(2)}, u32[]{:S(2)}) collective-permute-start(f32[16,64]{1,0:T(8,128)S(1)} %convolution_add_fusion.8), channel_id=1, source_target_pairs={{8,0},{9,1},{10,2},{11,3},{12,4},{13,5},{14,6},{15,7},{24,16},{25,... | collective-permute-start | bytes 12296 | tf_op jit(solution)/shard_map/ppermute | solution.py:10
  58.1 1.3 %collective-permute-start.22 = (f32[16,64]{1,0:T(8,128)S(1)}, f32[16,64]{1,0:T(8,128)S(1)}, u32[]{:S(2)}, u32[]{:S(2)}) collective-permute-start(f32[16,64]{1,0:T(8,128)S(1)} %convolution_add_fusion.8), channel_id=1, source_target_pairs={{12,0},{13,1},{14,2},{15,3},{28,16},{29,17},{30,18},{31,19}} | collective-permute-start | bytes 12296 | tf_op jit(solution)/shard_map/ppermute | solution.py:10
  59.4 5.8 %collective-permute-start.23 = (f32[16,64]{1,0:T(8,128)S(1)}, f32[16,64]{1,0:T(8,128)S(1)}, u32[]{:S(2)}, u32[]{:S(2)}) collective-permute-start(f32[16,64]{1,0:T(8,128)S(1)} %convolution_add_fusion.8), channel_id=1, source_target_pairs={{0,12},{1,13},{2,14},{3,15},{16,28},{17,29},{18,30},{19,31}} | collective-permute-start | bytes 12296 | tf_op jit(solution)/shard_map/ppermute | solution.py:10
  65.2 1.2 %convolution_bitcast_fusion.4 = f32[2,16,64]{2,1,0:T(8,128)S(1)} fusion(bf16[31,3,64,64]{3,2,1,0:T(8,128)(2,1)} %param.18, f32[2,3,16,64]{3,2,1,0:T(8,128)S(1)} %bitcast.124, f32[2,3]{1,0:T(2,128)S(1)} %copy.32), kind=kOutput, calls=%fused_computation.15 | convolution fusion | flops 4724736 | bytes 131096 | tf_op jit(solution)/shard_map/tkvr,tkrs->tvs/dot_general | solution.py:104
  66.4 3.7 %collective-permute-start.6 = (f32[3,16,64]{2,1,0:T(8,128)S(1)}, f32[3,16,64]{2,1,0:T(8,128)S(1)}, u32[]{:S(2)}, u32[]{:S(2)}) collective-permute-start(f32[3,16,64]{2,1,0:T(8,128)S(1)} %get-tuple-element.11), channel_id=1, source_target_pairs={{0,1},{1,2},{2,3},{3,4},{4,5},{5,6},{6,7},{7,8},{8,9},{9,10},{10,1... | collective-permute-start | bytes 36872 | tf_op jit(solution)/shard_map/ppermute | solution.py:10
  70.1 1.1 convolution_bitcast_fusion.7
  71.2 1.9 %collective-permute-start.7 = (f32[3,16,64]{2,1,0:T(8,128)S(1)}, f32[3,16,64]{2,1,0:T(8,128)S(1)}, u32[]{:S(2)}, u32[]{:S(2)}) collective-permute-start(f32[3,16,64]{2,1,0:T(8,128)S(1)} %get-tuple-element.12), channel_id=1, source_target_pairs={{1,0},{2,1},{3,2},{4,3},{5,4},{6,5},{7,6},{8,7},{9,8},{10,9},{11,1... | collective-permute-start | bytes 36872 | tf_op jit(solution)/shard_map/ppermute | solution.py:10
  73.1 3.6 %collective-permute-start.4 = (f32[3,16,64]{2,1,0:T(8,128)}, f32[3,16,64]{2,1,0:T(8,128)}, u32[]{:S(2)}, u32[]{:S(2)}) collective-permute-start(f32[3,16,64]{2,1,0:T(8,128)} %get-tuple-element.7), channel_id=1, source_target_pairs={{0,1},{1,2},{2,3},{3,4},{4,5},{5,6},{6,7},{7,8},{8,9},{9,10},{10,1... | collective-permute-start | bytes 36872 | tf_op jit(solution)/shard_map/ppermute | solution.py:10
  76.8 1.9 %collective-permute-start.5 = (f32[3,16,64]{2,1,0:T(8,128)}, f32[3,16,64]{2,1,0:T(8,128)}, u32[]{:S(2)}, u32[]{:S(2)}) collective-permute-start(f32[3,16,64]{2,1,0:T(8,128)} %get-tuple-element.8), channel_id=1, source_target_pairs={{1,0},{2,1},{3,2},{4,3},{5,4},{6,5},{7,6},{8,7},{9,8},{10,9},{11,1... | collective-permute-start | bytes 36872 | tf_op jit(solution)/shard_map/ppermute | solution.py:10
  78.7 3.6 %collective-permute-start.2 = (f32[3,16,64]{2,1,0:T(8,128)}, f32[3,16,64]{2,1,0:T(8,128)}, u32[]{:S(2)}, u32[]{:S(2)}) collective-permute-start(f32[3,16,64]{2,1,0:T(8,128)} %get-tuple-element.5), channel_id=1, source_target_pairs={{0,1},{1,2},{2,3},{3,4},{4,5},{5,6},{6,7},{7,8},{8,9},{9,10},{10,1... | collective-permute-start | bytes 36872 | tf_op jit(solution)/shard_map/ppermute | solution.py:10
  82.4 1.0 convolution_bitcast_fusion.6
  83.4 0.9 convolution_add_fusion.7
  84.3 0.9 convolution_add_fusion.6
  85.2 0.9 convolution_add_fusion.5
  86.0 1.6 %convolution_add_fusion.4 = f32[2,16,64]{2,1,0:T(8,128)} fusion(f32[2,16,64]{2,1,0:T(8,128)S(1)} %convolution_bitcast_fusion.4, bf16[30,64,64]{2,1,0:T(8,128)(2,1)} %param.17, f32[16,64]{1,0:T(8,128)S(1)} %convolution_add_fusion.5), kind=kOutput, calls=%fused_computation.14 | convolution fusion | flops 1574912 | bytes 53248 | tf_op jit(solution)/shard_map/tvs,trs->tvr/dot_general | solution.py:166
  87.6 1.9 %collective-permute-start.3 = (f32[3,16,64]{2,1,0:T(8,128)}, f32[3,16,64]{2,1,0:T(8,128)}, u32[]{:S(2)}, u32[]{:S(2)}) collective-permute-start(f32[3,16,64]{2,1,0:T(8,128)} %get-tuple-element.6), channel_id=1, source_target_pairs={{1,0},{2,1},{3,2},{4,3},{5,4},{6,5},{7,6},{8,7},{9,8},{10,9},{11,1... | collective-permute-start | bytes 36872 | tf_op jit(solution)/shard_map/ppermute | solution.py:10
  89.5 3.6 %collective-permute-start = (bf16[3,16,128]{2,1,0:T(8,128)(2,1)}, bf16[3,16,128]{2,1,0:T(8,128)(2,1)}, u32[]{:S(2)}, u32[]{:S(2)}) collective-permute-start(bf16[3,16,128]{2,1,0:T(8,128)(2,1)} %get-tuple-element.9), channel_id=1, source_target_pairs={{0,1},{1,2},{2,3},{3,4},{4,5},{5,6},{6,7},{7,8},{8,9},{9,10},{10,1... | collective-permute-start | bytes 36872 | tf_op jit(solution)/shard_map/ppermute | solution.py:10
  93.9 1.3 %convolution_bitcast_fusion.3 = f32[4,16,64]{2,1,0:T(8,128)S(1)} fusion(bf16[31,3,64,64]{3,2,1,0:T(8,128)(2,1)} %param.18, f32[4,3,16,64]{3,2,1,0:T(8,128)S(1)} %bitcast.122, f32[4,3]{1,0:T(4,128)} %copy.30), kind=kOutput, calls=%fused_computation.13 | convolution fusion | flops 9449472 | bytes 264192 | tf_op jit(solution)/shard_map/tkvr,tkrs->tvs/dot_general | solution.py:104
  95.9 1.0 convolution_add_fusion.3
  97.0 1.9 %collective-permute-start.1 = (bf16[3,16,128]{2,1,0:T(8,128)(2,1)}, bf16[3,16,128]{2,1,0:T(8,128)(2,1)S(1)}, u32[]{:S(2)}, u32[]{:S(2)}) collective-permute-start(bf16[3,16,128]{2,1,0:T(8,128)(2,1)} %get-tuple-element.10), channel_id=1, source_target_pairs={{1,0},{2,1},{3,2},{4,3},{5,4},{6,5},{7,6},{8,7},{9,8},{10,9},{11,1... | collective-permute-start | bytes 36872 | tf_op jit(solution)/shard_map/ppermute | solution.py:10
  99.7 1.4 %gather_fusion.2 = f32[24,16,64]{2,1,0:T(8,128)} fusion(f32[14,16,64]{2,1,0:T(8,128)S(1)} %pad_maximum_fusion.1, s32[1024]{0:T(1024)} %pad_clamp_fusion.2), kind=kCustom, calls=%fused_computation.2 | custom fusion | bytes 196704 | tf_op jit(solution)/shard_map/gather | solution.py:101
  101.1 1.7 %convolution_bitcast_fusion.2 = f32[8,16,64]{2,1,0:T(8,128)S(1)} fusion(bf16[31,3,64,64]{3,2,1,0:T(8,128)(2,1)} %param.18, f32[8,3,16,64]{3,2,1,0:T(8,128)} %bitcast.117, f32[8,3]{1,0:T(8,128)} %copy.28), kind=kOutput, calls=%fused_computation.11 | convolution fusion | flops 18898944 | bytes 626688 | tf_op jit(solution)/shard_map/tkvr,tkrs->tvs/dot_general | solution.py:104
  102.8 1.2 %convolution_add_fusion.2 = f32[8,16,64]{2,1,0:T(8,128)S(1)} fusion(f32[8,16,64]{2,1,0:T(8,128)S(1)} %convolution_bitcast_fusion.2, f32[8,16,64]{2,1,0:T(8,128)S(1)} %bitcast.123, bf16[30,64,64]{2,1,0:T(8,128)(2,1)} %param.17), kind=kOutput, calls=%fused_computation.10 | convolution fusion | flops 6299648 | bytes 229376 | tf_op jit(solution)/shard_map/tvs,trs->tvr/dot_general | solution.py:166
  104.8 1.6 %gather_fusion.1 = f32[48,16,64]{2,1,0:T(8,128)} fusion(f32[22,16,64]{2,1,0:T(8,128)S(1)} %pad_maximum_fusion, s32[1024]{0:T(1024)} %pad_clamp_fusion.3), kind=kCustom, calls=%fused_computation.1 | custom fusion | bytes 393408 | tf_op jit(solution)/shard_map/gather | solution.py:101
  106.4 2.2 %convolution_bitcast_fusion = f32[16,16,64]{2,1,0:T(8,128)S(1)} fusion(bf16[31,3,64,64]{3,2,1,0:T(8,128)(2,1)} %param.18, f32[16,3,16,64]{3,2,1,0:T(8,128)} %bitcast.111, f32[16,3]{1,0:T(8,128)S(1)} %copy-done.12), kind=kOutput, calls=%fused_computation.7 | convolution fusion | flops 37797888 | bytes 1245376 | tf_op jit(solution)/shard_map/tkvr,tkrs->tvs/dot_general | solution.py:104
  110.0 1.4 %gather_fusion = bf16[96,16,128]{2,1,0:T(8,128)(2,1)} fusion(bf16[22,16,128]{2,1,0:T(8,128)(2,1)S(1)} %pad_maximum_fusion.2, s32[1024]{0:T(1024)S(1)} %copy-done.11), kind=kCustom, calls=%fused_computation | custom fusion | bytes 786816 | tf_op jit(solution)/shard_map/gather | solution.py:87
  111.4 1.6 %convolution_bitcast_fusion.1 = f32[16,16,128]{2,1,0:T(8,128)S(1)} fusion(bf16[16,6,128,128]{3,2,1,0:T(8,128)(2,1)S(1)} %copy-done, bf16[16,6,16,128]{3,2,1,0:T(8,128)(2,1)} %bitcast.112, bf16[16,6]{1,0:T(8,128)(2,1)S(1)} %copy-done.13), kind=kOutput, calls=%fused_computation.8 | convolution fusion | flops 50528256 | bytes 3670208 | tf_op jit(solution)/shard_map/ikvp,ikpq->ivq/dot_general | solution.py:88
  113.0 1.0 fusion
  (118 shorter events, 15.5 us)
Async XLA Ops:
  0.0 111.4 %copy-start = (bf16[16,6,128,128]{3,2,1,0:T(8,128)(2,1)S(1)}, bf16[16,6,128,128]{3,2,1,0:T(8,128)(2,1)}, u32[]{:S(2)}) copy-start(bf16[16,6,128,128]{3,2,1,0:T(8,128)(2,1)} %param.14) | copy-start | bytes 9437188
  0.0 2.2 %slice-start = ((bf16[30,64,64]{2,1,0:T(8,128)(2,1)}), bf16[16,64,64]{2,1,0:T(8,128)(2,1)S(1)}, s32[]{:S(2)}) async-start(bf16[30,64,64]{2,1,0:T(8,128)(2,1)} %param.17), calls=%async_computation | async-start | bytes 524288 | tf_op jit(solution)/shard_map/slice | solution.py:55
  0.0 2.6 %slice-start.1 = ((bf16[30,64,64]{2,1,0:T(8,128)(2,1)}), bf16[8,64,64]{2,1,0:T(8,128)(2,1)S(1)}, s32[]{:S(2)}) async-start(bf16[30,64,64]{2,1,0:T(8,128)(2,1)} %param.17), calls=%async_computation.1 | async-start | bytes 262144 | tf_op jit(solution)/shard_map/slice | solution.py:55
  0.0 2.9 %slice-start.2 = ((bf16[30,64,64]{2,1,0:T(8,128)(2,1)}), bf16[4,64,64]{2,1,0:T(8,128)(2,1)S(1)}, s32[]{:S(2)}) async-start(bf16[30,64,64]{2,1,0:T(8,128)(2,1)} %param.17), calls=%async_computation.2 | async-start | bytes 131072 | tf_op jit(solution)/shard_map/slice | solution.py:55
  0.0 3.1 %copy-start.1 = (bf16[30,64,64]{2,1,0:T(8,128)(2,1)S(1)}, bf16[30,64,64]{2,1,0:T(8,128)(2,1)}, u32[]{:S(2)}) copy-start(bf16[30,64,64]{2,1,0:T(8,128)(2,1)} %param.17) | copy-start | bytes 737284
  0.0 13.8 %copy-start.9 = (s32[31,3]{0,1:T(4,128)S(1)}, s32[31,3]{0,1:T(4,128)}, u32[]{:S(2)}) copy-start(s32[31,3]{0,1:T(4,128)} %param.20) | copy-start | bytes 1120
  0.0 16.9 %copy-start.10 = (s32[31,3]{0,1:T(4,128)S(1)}, s32[31,3]{0,1:T(4,128)}, u32[]{:S(2)}) copy-start(s32[31,3]{0,1:T(4,128)} %param.19) | copy-start | bytes 1120
  0.1 21.2 %copy-start.15 = (s32[16,6]{0,1:T(8,128)S(1)}, s32[16,6]{0,1:T(8,128)}, u32[]{:S(2)}) copy-start(s32[16,6]{0,1:T(8,128)} %param.15) | copy-start | bytes 1156
  0.1 24.1 %copy-start.14 = (s32[16,6]{0,1:T(8,128)S(1)}, s32[16,6]{0,1:T(8,128)}, u32[]{:S(2)}) copy-start(s32[16,6]{0,1:T(8,128)} %param.16) | copy-start | bytes 1156
  1.4 1.9 %copy-start.3 = (f32[16,16,64]{2,1,0:T(8,128)}, f32[16,16,64]{2,1,0:T(8,128)S(1)}, u32[]{:S(2)}) copy-start(f32[16,16,64]{2,1,0:T(8,128)S(1)} %fusion.91) | copy-start | bytes 196612
  2.6 0.8 copy-start.6
  3.3 21.6 %collective-permute-start.14 = (f32[16,64]{1,0:T(8,128)S(1)}, f32[16,64]{1,0:T(8,128)S(1)}, u32[]{:S(2)}, u32[]{:S(2)}) collective-permute-start(f32[16,64]{1,0:T(8,128)S(1)} %convolution_bitcast_fusion.9), channel_id=1, source_target_pairs={{0,1},{1,0},{2,3},{3,2},{4,5},{5,4},{6,7},{7,6},{8,9},{9,8},{10,11... | collective-permute-start | bytes 12296 | tf_op jit(solution)/shard_map/ppermute | solution.py:20
  3.4 28.1 %collective-permute-start.10 = (f32[16,64]{1,0:T(8,128)S(1)}, f32[16,64]{1,0:T(8,128)S(1)}, u32[]{:S(2)}, u32[]{:S(2)}) collective-permute-start(f32[16,64]{1,0:T(8,128)S(1)} %convolution_bitcast_fusion.9), channel_id=1, source_target_pairs={{0,3},{1,4},{2,5},{3,6},{4,7},{5,8},{6,9},{7,10},{8,11},{9,12},{10... | collective-permute-start | bytes 12296 | tf_op jit(solution)/shard_map/ppermute | solution.py:10
  7.9 91.0 %copy-start.7 = (f32[8,16,64,1]{2,1,3,0:T(8,128)S(1)}, f32[8,16,64,1]{2,1,3,0:T(8,128)}, u32[]{:S(2)}) copy-start(f32[8,16,64,1]{2,1,3,0:T(8,128)} %copy-done.6) | copy-start | bytes 98308
  7.9 25.4 %collective-permute-start.11 = (f32[16,64]{1,0:T(8,128)S(1)}, f32[16,64]{1,0:T(8,128)S(1)}, u32[]{:S(2)}, u32[]{:S(2)}) collective-permute-start(f32[16,64]{1,0:T(8,128)S(1)} %convolution_bitcast_fusion.9), channel_id=1, source_target_pairs={{0,2},{1,3},{2,4},{3,5},{4,6},{5,7},{6,8},{7,9},{8,10},{9,11},{10,... | collective-permute-start | bytes 12296 | tf_op jit(solution)/shard_map/ppermute | solution.py:10
  11.2 25.0 %collective-permute-start.12 = (f32[16,64]{1,0:T(8,128)S(1)}, f32[16,64]{1,0:T(8,128)S(1)}, u32[]{:S(2)}, u32[]{:S(2)}) collective-permute-start(f32[16,64]{1,0:T(8,128)S(1)} %convolution_bitcast_fusion.9), channel_id=1, source_target_pairs={{2,0},{3,1},{4,2},{5,3},{6,4},{7,5},{8,6},{9,7},{10,8},{11,9},{12,... | collective-permute-start | bytes 12296 | tf_op jit(solution)/shard_map/ppermute | solution.py:10
  12.5 26.9 %collective-permute-start.13 = (f32[16,64]{1,0:T(8,128)S(1)}, f32[16,64]{1,0:T(8,128)S(1)}, u32[]{:S(2)}, u32[]{:S(2)}) collective-permute-start(f32[16,64]{1,0:T(8,128)S(1)} %convolution_bitcast_fusion.9), channel_id=1, source_target_pairs={{3,0},{4,1},{5,2},{6,3},{7,4},{8,5},{9,6},{10,7},{11,8},{12,9},{13... | collective-permute-start | bytes 12296 | tf_op jit(solution)/shard_map/ppermute | solution.py:10
  24.9 20.8 %collective-permute-start.8 = (f32[2,16,64]{2,1,0:T(8,128)S(1)}, f32[2,16,64]{2,1,0:T(8,128)S(1)}, u32[]{:S(2)}, u32[]{:S(2)}) collective-permute-start(f32[2,16,64]{2,1,0:T(8,128)S(1)} %convolution_bitcast_fusion.5), channel_id=1, source_target_pairs={{0,1},{1,2},{2,3},{3,4},{4,5},{5,6},{6,7},{7,8},{8,9},{9,10},{10,1... | collective-permute-start | bytes 24584 | tf_op jit(solution)/shard_map/ppermute | solution.py:10
  31.4 19.7 %collective-permute-start.9 = (f32[2,16,64]{2,1,0:T(8,128)S(1)}, f32[2,16,64]{2,1,0:T(8,128)S(1)}, u32[]{:S(2)}, u32[]{:S(2)}) collective-permute-start(f32[2,16,64]{2,1,0:T(8,128)S(1)} %convolution_bitcast_fusion.5), channel_id=1, source_target_pairs={{1,0},{2,1},{3,2},{4,3},{5,4},{6,5},{7,6},{8,7},{9,8},{10,9},{11,1... | collective-permute-start | bytes 24584 | tf_op jit(solution)/shard_map/ppermute | solution.py:10
  33.4 9.3 %collective-permute-start.19 = (f32[16,64]{1,0:T(8,128)S(1)}, f32[16,64]{1,0:T(8,128)S(1)}, u32[]{:S(2)}, u32[]{:S(2)}) collective-permute-start(f32[16,64]{1,0:T(8,128)S(1)} %convolution_add_fusion.9), channel_id=1, source_target_pairs={{0,2},{2,0},{1,3},{3,1},{4,6},{6,4},{5,7},{7,5},{8,10},{10,8},{9,1... | collective-permute-start | bytes 12296 | tf_op jit(solution)/shard_map/ppermute | solution.py:20
  36.2 20.5 %collective-permute-start.15 = (f32[16,64]{1,0:T(8,128)S(1)}, f32[16,64]{1,0:T(8,128)S(1)}, u32[]{:S(2)}, u32[]{:S(2)}) collective-permute-start(f32[16,64]{1,0:T(8,128)S(1)} %convolution_add_fusion.9), channel_id=1, source_target_pairs={{0,4},{1,5},{2,6},{3,7},{4,8},{5,9},{6,10},{7,11},{8,12},{9,13},{1... | collective-permute-start | bytes 12296 | tf_op jit(solution)/shard_map/ppermute | solution.py:10
  39.4 18.6 %collective-permute-start.16 = (f32[16,64]{1,0:T(8,128)S(1)}, f32[16,64]{1,0:T(8,128)S(1)}, u32[]{:S(2)}, u32[]{:S(2)}) collective-permute-start(f32[16,64]{1,0:T(8,128)S(1)} %convolution_add_fusion.9), channel_id=1, source_target_pairs={{4,0},{5,1},{6,2},{7,3},{8,4},{9,5},{10,6},{11,7},{12,8},{13,9},{1... | collective-permute-start | bytes 12296 | tf_op jit(solution)/shard_map/ppermute | solution.py:10
  42.7 16.7 %collective-permute-start.17 = (f32[16,64]{1,0:T(8,128)S(1)}, f32[16,64]{1,0:T(8,128)S(1)}, u32[]{:S(2)}, u32[]{:S(2)}) collective-permute-start(f32[16,64]{1,0:T(8,128)S(1)} %convolution_add_fusion.9), channel_id=1, source_target_pairs={{6,0},{7,1},{8,2},{9,3},{10,4},{11,5},{12,6},{13,7},{14,8},{15,9},... | collective-permute-start | bytes 12296 | tf_op jit(solution)/shard_map/ppermute | solution.py:10
  45.7 20.7 %collective-permute-start.18 = (f32[16,64]{1,0:T(8,128)S(1)}, f32[16,64]{1,0:T(8,128)}, u32[]{:S(2)}, u32[]{:S(2)}) collective-permute-start(f32[16,64]{1,0:T(8,128)S(1)} %convolution_add_fusion.9), channel_id=1, source_target_pairs={{0,6},{1,7},{2,8},{3,9},{4,10},{5,11},{6,12},{7,13},{8,14},{9,15},... | collective-permute-start | bytes 12296 | tf_op jit(solution)/shard_map/ppermute | solution.py:10
  51.1 20.0 %collective-permute-start.20 = (f32[16,64]{1,0:T(8,128)S(1)}, f32[16,64]{1,0:T(8,128)}, u32[]{:S(2)}, u32[]{:S(2)}) collective-permute-start(f32[16,64]{1,0:T(8,128)S(1)} %convolution_add_fusion.8), channel_id=1, source_target_pairs={{0,8},{1,9},{2,10},{3,11},{4,12},{5,13},{6,14},{7,15},{16,24},{17,... | collective-permute-start | bytes 12296 | tf_op jit(solution)/shard_map/ppermute | solution.py:10
  56.7 16.4 %collective-permute-start.21 = (f32[16,64]{1,0:T(8,128)S(1)}, f32[16,64]{1,0:T(8,128)S(1)}, u32[]{:S(2)}, u32[]{:S(2)}) collective-permute-start(f32[16,64]{1,0:T(8,128)S(1)} %convolution_add_fusion.8), channel_id=1, source_target_pairs={{8,0},{9,1},{10,2},{11,3},{12,4},{13,5},{14,6},{15,7},{24,16},{25,... | collective-permute-start | bytes 12296 | tf_op jit(solution)/shard_map/ppermute | solution.py:10
  58.1 7.1 %copy-start.16 = (f32[16,64]{1,0:T(8,128)}, f32[16,64]{1,0:T(8,128)S(1)}, u32[]{:S(2)}) copy-start(f32[16,64]{1,0:T(8,128)S(1)} %collective-permute-done.16) | copy-start | bytes 12292
  58.1 18.7 %collective-permute-start.22 = (f32[16,64]{1,0:T(8,128)S(1)}, f32[16,64]{1,0:T(8,128)S(1)}, u32[]{:S(2)}, u32[]{:S(2)}) collective-permute-start(f32[16,64]{1,0:T(8,128)S(1)} %convolution_add_fusion.8), channel_id=1, source_target_pairs={{12,0},{13,1},{14,2},{15,3},{28,16},{29,17},{30,18},{31,19}} | collective-permute-start | bytes 12296 | tf_op jit(solution)/shard_map/ppermute | solution.py:10
  59.4 5.8 %copy-start.17 = (f32[16,64]{1,0:T(8,128)}, f32[16,64]{1,0:T(8,128)S(1)}, u32[]{:S(2)}) copy-start(f32[16,64]{1,0:T(8,128)S(1)} %collective-permute-done.17) | copy-start | bytes 12292
  59.4 19.4 %collective-permute-start.23 = (f32[16,64]{1,0:T(8,128)S(1)}, f32[16,64]{1,0:T(8,128)S(1)}, u32[]{:S(2)}, u32[]{:S(2)}) collective-permute-start(f32[16,64]{1,0:T(8,128)S(1)} %convolution_add_fusion.8), channel_id=1, source_target_pairs={{0,12},{1,13},{2,14},{3,15},{16,28},{17,29},{18,30},{19,31}} | collective-permute-start | bytes 12296 | tf_op jit(solution)/shard_map/ppermute | solution.py:10
  66.4 37.6 %copy-start.4 = (f32[16,16,64]{2,1,0:T(8,128)S(1)}, f32[16,16,64]{2,1,0:T(8,128)}, u32[]{:S(2)}) copy-start(f32[16,16,64]{2,1,0:T(8,128)} %copy-done.3) | copy-start | bytes 196612
  66.4 21.2 %collective-permute-start.6 = (f32[3,16,64]{2,1,0:T(8,128)S(1)}, f32[3,16,64]{2,1,0:T(8,128)S(1)}, u32[]{:S(2)}, u32[]{:S(2)}) collective-permute-start(f32[3,16,64]{2,1,0:T(8,128)S(1)} %get-tuple-element.11), channel_id=1, source_target_pairs={{0,1},{1,2},{2,3},{3,4},{4,5},{5,6},{6,7},{7,8},{8,9},{9,10},{10,1... | collective-permute-start | bytes 36872 | tf_op jit(solution)/shard_map/ppermute | solution.py:10
  71.2 18.3 %collective-permute-start.7 = (f32[3,16,64]{2,1,0:T(8,128)S(1)}, f32[3,16,64]{2,1,0:T(8,128)S(1)}, u32[]{:S(2)}, u32[]{:S(2)}) collective-permute-start(f32[3,16,64]{2,1,0:T(8,128)S(1)} %get-tuple-element.12), channel_id=1, source_target_pairs={{1,0},{2,1},{3,2},{4,3},{5,4},{6,5},{7,6},{8,7},{9,8},{10,9},{11,1... | collective-permute-start | bytes 36872 | tf_op jit(solution)/shard_map/ppermute | solution.py:10
  73.1 23.8 %collective-permute-start.4 = (f32[3,16,64]{2,1,0:T(8,128)}, f32[3,16,64]{2,1,0:T(8,128)}, u32[]{:S(2)}, u32[]{:S(2)}) collective-permute-start(f32[3,16,64]{2,1,0:T(8,128)} %get-tuple-element.7), channel_id=1, source_target_pairs={{0,1},{1,2},{2,3},{3,4},{4,5},{5,6},{6,7},{7,8},{8,9},{9,10},{10,1... | collective-permute-start | bytes 36872 | tf_op jit(solution)/shard_map/ppermute | solution.py:10
  76.8 22.1 %collective-permute-start.5 = (f32[3,16,64]{2,1,0:T(8,128)}, f32[3,16,64]{2,1,0:T(8,128)}, u32[]{:S(2)}, u32[]{:S(2)}) collective-permute-start(f32[3,16,64]{2,1,0:T(8,128)} %get-tuple-element.8), channel_id=1, source_target_pairs={{1,0},{2,1},{3,2},{4,3},{5,4},{6,5},{7,6},{8,7},{9,8},{10,9},{11,1... | collective-permute-start | bytes 36872 | tf_op jit(solution)/shard_map/ppermute | solution.py:10
  78.7 25.2 %collective-permute-start.2 = (f32[3,16,64]{2,1,0:T(8,128)}, f32[3,16,64]{2,1,0:T(8,128)}, u32[]{:S(2)}, u32[]{:S(2)}) collective-permute-start(f32[3,16,64]{2,1,0:T(8,128)} %get-tuple-element.5), channel_id=1, source_target_pairs={{0,1},{1,2},{2,3},{3,4},{4,5},{5,6},{6,7},{7,8},{8,9},{9,10},{10,1... | collective-permute-start | bytes 36872 | tf_op jit(solution)/shard_map/ppermute | solution.py:10
  87.6 16.4 %collective-permute-start.3 = (f32[3,16,64]{2,1,0:T(8,128)}, f32[3,16,64]{2,1,0:T(8,128)}, u32[]{:S(2)}, u32[]{:S(2)}) collective-permute-start(f32[3,16,64]{2,1,0:T(8,128)} %get-tuple-element.6), channel_id=1, source_target_pairs={{1,0},{2,1},{3,2},{4,3},{5,4},{6,5},{7,6},{8,7},{9,8},{10,9},{11,1... | collective-permute-start | bytes 36872 | tf_op jit(solution)/shard_map/ppermute | solution.py:10
  89.5 19.7 %collective-permute-start = (bf16[3,16,128]{2,1,0:T(8,128)(2,1)}, bf16[3,16,128]{2,1,0:T(8,128)(2,1)}, u32[]{:S(2)}, u32[]{:S(2)}) collective-permute-start(bf16[3,16,128]{2,1,0:T(8,128)(2,1)} %get-tuple-element.9), channel_id=1, source_target_pairs={{0,1},{1,2},{2,3},{3,4},{4,5},{5,6},{6,7},{7,8},{8,9},{9,10},{10,1... | collective-permute-start | bytes 36872 | tf_op jit(solution)/shard_map/ppermute | solution.py:10
  95.9 10.5 %copy-start.12 = (f32[16,3]{1,0:T(8,128)S(1)}, f32[16,3]{1,0:T(8,128)}, u32[]{:S(2)}) copy-start(f32[16,3]{1,0:T(8,128)} %copy.26) | copy-start | bytes 580
  97.0 12.2 %collective-permute-start.1 = (bf16[3,16,128]{2,1,0:T(8,128)(2,1)}, bf16[3,16,128]{2,1,0:T(8,128)(2,1)S(1)}, u32[]{:S(2)}, u32[]{:S(2)}) collective-permute-start(bf16[3,16,128]{2,1,0:T(8,128)(2,1)} %get-tuple-element.10), channel_id=1, source_target_pairs={{1,0},{2,1},{3,2},{4,3},{5,4},{6,5},{7,6},{8,7},{9,8},{10,9},{11,1... | collective-permute-start | bytes 36872 | tf_op jit(solution)/shard_map/ppermute | solution.py:10
  104.8 4.4 %copy-start.8 = (bf16[16,16,128]{2,1,0:T(8,128)(2,1)S(1)}, bf16[16,16,128]{2,1,0:T(8,128)(2,1)}, u32[]{:S(2)}) copy-start(bf16[16,16,128]{2,1,0:T(8,128)(2,1)} %param.12) | copy-start | bytes 196612
  104.8 5.1 %copy-start.11 = (s32[1024]{0:T(1024)S(1)}, s32[1024]{0:T(1024)}, u32[]{:S(2)}) copy-start(s32[1024]{0:T(1024)} %pad_clamp_fusion.4) | copy-start | bytes 12292
  106.4 2.2 %copy-start.2 = (bf16[30,64,64]{2,1,0:T(8,128)(2,1)S(1)}, bf16[30,64,64]{2,1,0:T(8,128)(2,1)}, u32[]{:S(2)}) copy-start(bf16[30,64,64]{2,1,0:T(8,128)(2,1)} %param.17) | copy-start | bytes 737284
  106.4 4.9 %copy-start.13 = (bf16[16,6]{1,0:T(8,128)(2,1)S(1)}, bf16[16,6]{1,0:T(8,128)(2,1)}, u32[]{:S(2)}) copy-start(bf16[16,6]{1,0:T(8,128)(2,1)} %copy.24) | copy-start | bytes 580
  111.4 1.6 %copy-start.5 = (bf16[16,64,128]{2,1,0:T(8,128)(2,1)S(1)}, bf16[16,64,128]{2,1,0:T(8,128)(2,1)}, u32[]{:S(2)}) copy-start(bf16[16,64,128]{2,1,0:T(8,128)(2,1)} %param.13) | copy-start | bytes 786436
where the time goes:
time: 116 us; the launch traced here: 114 us
  starting transfers between devices  67 us (58%)
  matrix products  25.7 us (22%)
  local copies, waits for them, and re-layouts  15 us (13%)
  other arithmetic  5.51 us (5%)
    ppermute x22, starting transfers between devices, from_behind(): return lax.ppermute(shard, axis, pairs)  64.1 us
    dot_general x4, matrix products, per_device(): jnp.einsum('tkvr,tkrs->tvs', gathered, matrix_stack, precision=highest_le...  6.38 us
    dot_general x4, matrix products, per_device(): jnp.einsum('tvs,trs->tvr', spread, matrix_stack, precision=highest_level)  4.33 us
    gather x4, local copies, waits for them, and re-layouts, per_device(): gathered = around_coef[spot_rows] * in_use[:, :, None, None]  4.21 us
    dot_general x3, matrix products, per_device(): jnp.einsum('kvr,krs->vs', chosen, top_matrix_stack, precision=highest_level)  3.05 us
    ppermute x2, starting transfers between devices, from_partner(): return lax.ppermute(block, axis, route)  2.9 us
    slice x3, local copies, waits for them, and re-layouts, per_device(): level_list[height][level_list[height].shape[0] - rim_counts[height]:]  2.75 us
    dot_general x3, matrix products, per_device(): jnp.dot(downward, own_mat.T, precision=highest_level)  2.61 us
  transfers between devices with their start and end apart: 24, of which 0 were waited for; matrix products, arithmetic and copies ran while one was open for 33% of the time, Pallas kernels for 0%

commit v1 on v0

v1 whole, which is shorter than its diff:
```python
import functools

import jax
import jax.numpy as jnp
from jax import lax
from jax.experimental import pallas as pl
from jax.experimental.pallas import tpu as pltpu
from jax.sharding import PartitionSpec as P

RIM = 2
MESH = pl.DeviceIdType.MESH
F32 = jnp.float32
BF16 = jnp.bfloat16


def bdot(left, right, transposed=False):
    contract = 2 if transposed else 1
    return lax.dot_general(
        left, right, (((2,), (contract,)), ((0,), (0,))), preferred_element_type=F32
    )


def split(value):
    high = value.astype(BF16)
    low = (value - high.astype(F32)).astype(BF16)
    return high, low


def stacked(value):
    return jnp.concatenate(split(value), axis=-2)


def folded(value):
    half = value.shape[-2] // 2
    return value[..., :half, :] + value[..., half:, :]


def kernel(
    sizes,
    near_list,
    near_mask,
    far_list,
    far_mask,
    vectors,
    basis,
    near_blocks,
    transfer_low,
    coupling_low,
    transfer_top,
    coupling_top,
    out,
    vec_buf,
    basis_buf,
    near_buf,
    tlow_buf,
    clow_buf,
    ttop_buf,
    ctop_buf,
    near_acc,
    far_acc,
    roots,
    *rest,
):
    leaves, low_levels, tree_devs, num_sub, top_used, k_near, k_far = sizes
    level_bufs = rest[: low_levels - 1]
    top_bufs = rest[low_levels - 1 : low_levels - 1 + top_used]
    local_sem, rim_send, rim_recv, root_send, root_recv = rest[-5:]
    leaf_at = lax.axis_index("leaf")
    device = leaf_at * num_sub + lax.axis_index("sub")
    copy_at = lax.axis_index("copies")

    def place(index):
        return (copy_at, index // num_sub, index % num_sub)

    barrier = pltpu.get_barrier_semaphore()

    def greet(step, carry):
        pl.semaphore_signal(
            barrier, inc=1, device_id=place((device + step) % tree_devs), device_id_type=MESH
        )
        return carry

    lax.fori_loop(1, tree_devs, greet, 0, unroll=tree_devs <= 16)

    moves = [
        (vectors, vec_buf.at[pl.ds(RIM, leaves)]),
        (basis, basis_buf),
        (transfer_low, tlow_buf),
        (near_blocks, near_buf),
        (coupling_low, clow_buf),
        (transfer_top, ttop_buf),
    ]
    for height in range(1, top_used + 1):
        row = tree_devs - 2 * (tree_devs >> height) + device // (1 << height)
        moves.append((coupling_top.at[row], ctop_buf.at[height - 1]))
    copies = [
        pltpu.make_async_copy(source, target, local_sem.at[at])
        for at, (source, target) in enumerate(moves)
    ]
    for copy in copies:
        copy.start()

    starts = [2 * leaves - 2 * (leaves >> height) for height in range(low_levels)]
    counts = [leaves >> height for height in range(low_levels)]
    rims = [min(RIM, count) for count in counts]

    vec_buf[leaves + 2 * RIM] = jnp.zeros(vec_buf.shape[1:], BF16)
    for buf in level_bufs:
        buf[buf.shape[0] - 1] = jnp.zeros(buf.shape[1:], BF16)
    for buf in top_bufs:
        buf[buf.shape[0] - 1] = jnp.zeros(buf.shape[1:], BF16)
    roots[tree_devs] = jnp.zeros(roots.shape[1:], BF16)

    def rim_copies(buf, count, rim, at):
        to_right = pltpu.make_async_remote_copy(
            src_ref=buf.at[pl.ds(count, rim)],
            dst_ref=buf.at[pl.ds(0, rim)],
            send_sem=rim_send.at[2 * at],
            recv_sem=rim_recv.at[2 * at],
            device_id=place(device + 1),
            device_id_type=MESH,
        )
        to_left = pltpu.make_async_remote_copy(
            src_ref=buf.at[pl.ds(rim, rim)],
            dst_ref=buf.at[pl.ds(rim + count, rim)],
            send_sem=rim_send.at[2 * at + 1],
            recv_sem=rim_recv.at[2 * at + 1],
            device_id=place(device - 1),
            device_id_type=MESH,
        )
        return to_right, to_left

    rim_pairs = [rim_copies(vec_buf, leaves, RIM, low_levels - 1)]
    for height in range(low_levels - 1):
        rim_pairs.append(rim_copies(level_bufs[height], counts[height], rims[height], height))

    has_right = device < tree_devs - 1
    has_left = device > 0

    def send_rims(at):
        to_right, to_left = rim_pairs[at]

        @pl.when(has_right)
        def _():
            to_right.start()

        @pl.when(has_left)
        def _():
            to_left.start()

    def take_rims(at):
        to_right, to_left = rim_pairs[at]

        @pl.when(has_left)
        def _():
            to_right.wait_recv()

        @pl.when(has_right)
        def _():
            to_left.wait_recv()

    copies[0].wait()
    copies[1].wait()
    coefs = bdot(vec_buf[pl.ds(RIM, leaves)], basis_buf[...], transposed=True)
    pieces = stacked(coefs)
    level_bufs[0][pl.ds(rims[0], counts[0])] = pieces
    pl.semaphore_wait(barrier, tree_devs - 1)
    send_rims(0)
    send_rims(1)
    copies[2].wait()
    for height in range(1, low_levels):
        below = counts[height - 1]
        moved = folded(bdot(pieces, tlow_buf[pl.ds(starts[height - 1], below)]))
        moved = moved.reshape((below // 2, 2) + moved.shape[1:])
        coefs = moved[:, 0] + moved[:, 1]
        if height < low_levels - 1:
            pieces = stacked(coefs)
            level_bufs[height][pl.ds(rims[height], counts[height])] = pieces
            send_rims(height + 1)
    high, low = split(coefs[0])
    roots[device] = jnp.concatenate([high.astype(F32), low.astype(F32)], axis=-1).astype(BF16)

    def send_root(step, carry):
        pltpu.make_async_remote_copy(
            src_ref=roots.at[device],
            dst_ref=roots.at[device],
            send_sem=root_send,
            recv_sem=root_recv,
            device_id=place((device + step) % tree_devs),
            device_id_type=MESH,
        ).start()
        return carry

    lax.fori_loop(1, tree_devs, send_root, 0, unroll=tree_devs <= 16)

    take_rims(0)
    copies[3].wait()
    near_base = device * leaves - RIM

    def near_step(leaf, carry):
        sources = []
        for slot in range(k_near):
            spot = jnp.where(
                near_mask[leaf, slot] != 0,
                near_list[leaf, slot] - near_base,
                leaves + 2 * RIM,
            )
            sources.append(vec_buf[spot])
        blocks = near_buf[leaf]
        near_acc[leaf] = jnp.dot(
            jnp.concatenate(sources, axis=-1),
            blocks.reshape(blocks.shape[0] * blocks.shape[1], blocks.shape[2]),
            preferred_element_type=F32,
        )
        return carry

    lax.fori_loop(0, leaves, near_step, 0, unroll=True)

    copies[4].wait()
    for height in range(low_levels - 1):
        take_rims(height + 1)
        buf = level_bufs[height]
        far_base = device * counts[height] - rims[height]
        zero_spot = buf.shape[0] - 1

        def far_step(box, carry, buf=buf, far_base=far_base, zero_spot=zero_spot, height=height):
            row = starts[height] + box
            total = None
            for slot in range(k_far):
                spot = jnp.where(
                    far_mask[row, slot] != 0, far_list[row, slot] - far_base, zero_spot
                )
                term = jnp.dot(buf[spot], clow_buf[row, slot], preferred_element_type=F32)
                total = term if total is None else total + term
            far_acc[row] = folded(total)
            return carry

        lax.fori_loop(0, counts[height], far_step, 0, unroll=True)

    for copy in copies[5:]:
        copy.wait()
    arrived = roots.at[pl.ds(0, tree_devs - 1)]
    pltpu.make_async_copy(arrived, arrived, root_recv).wait()

    def doubled(matrix):
        return jnp.concatenate([matrix, matrix], axis=-2)

    pieces = roots[pl.ds(0, tree_devs)]
    for height in range(1, top_used + 1):
        below = tree_devs >> (height - 1)
        first = 2 * tree_devs - 2 * below
        mats = ttop_buf[pl.ds(first, below)]
        moved = bdot(pieces, doubled(mats)) if height == 1 else folded(bdot(pieces, mats))
        moved = moved.reshape((below // 2, 2) + moved.shape[1:])
        pieces = stacked(moved[:, 0] + moved[:, 1])
        top_bufs[height - 1][pl.ds(0, below // 2)] = pieces

    root_row = starts[low_levels - 1]
    downward = None
    for height in range(top_used, -1, -1):
        node = device // (1 << height)
        boxes = tree_devs >> height
        total = None
        if height == 0:
            for slot in range(k_far):
                spot = jnp.where(
                    far_mask[root_row, slot] != 0, far_list[root_row, slot], tree_devs
                )
                term = jnp.dot(
                    roots[spot], doubled(clow_buf[root_row, slot]), preferred_element_type=F32
                )
                total = term if total is None else total + term
        else:
            odd = node % 2
            for slot, (even_step, odd_step) in enumerate(((-2, -3), (2, -2), (3, 2))):
                source = node + jnp.where(odd == 1, odd_step, even_step)
                spot = jnp.where((source >= 0) & (source < boxes), source, boxes)
                term = jnp.dot(
                    top_bufs[height - 1][spot],
                    ctop_buf[height - 1, slot],
                    preferred_element_type=F32,
                )
                total = term if total is None else total + term
            total = folded(total)
        if downward is not None:
            matrix = ttop_buf[2 * tree_devs - 2 * boxes + node]
            total = total + folded(
                lax.dot_general(
                    stacked(downward), matrix, (((1,), (1,)), ((), ())), preferred_element_type=F32
                )
            )
        downward = total

    expanded = downward[None]
    for height in range(low_levels - 2, -1, -1):
        count = counts[height]
        spread = stacked(expanded)
        spread = jnp.broadcast_to(spread[:, None], (count // 2, 2) + spread.shape[1:])
        spread = spread.reshape((count,) + spread.shape[2:])
        mats = tlow_buf[pl.ds(starts[height], count)]
        expanded = far_acc[pl.ds(starts[height], count)] + folded(
            bdot(spread, mats, transposed=True)
        )
    leaf_term = folded(bdot(stacked(expanded), basis_buf[...]))
    out[...] = (near_acc[...] + leaf_term).astype(out.dtype)

    sent = roots.at[pl.ds(0, tree_devs - 1)]
    pltpu.make_async_copy(sent, sent, root_send).wait()
    for to_right, to_left in rim_pairs:

        @pl.when(has_right)
        def _(to_right=to_right):
            to_right.wait_send()

        @pl.when(has_left)
        def _(to_left=to_left):
            to_left.wait_send()


def per_device(
    vectors,
    leaf_basis,
    near_blocks,
    near_list,
    near_mask,
    transfer_low,
    coupling_low,
    far_list,
    far_mask,
    transfer_top,
    coupling_top,
):
    tree_devs = lax.axis_size(("leaf", "sub"))
    num_sub = lax.axis_size("sub")
    leaves, num_vectors, points = vectors.shape
    rank = leaf_basis.shape[1]
    k_near = near_blocks.shape[1]
    k_far = coupling_low.shape[1]
    low_levels = leaves.bit_length()
    top_used = max(tree_devs.bit_length() - 3, 0)
    counts = [leaves >> height for height in range(low_levels - 1)]
    boxes = [
        pltpu.VMEM((count + 2 * min(RIM, count) + 1, 2 * num_vectors, rank), BF16)
        for count in counts
    ] + [
        pltpu.VMEM(((tree_devs >> height) + 1, 2 * num_vectors, rank), BF16)
        for height in range(1, top_used + 1)
    ]
    scratch = [
        pltpu.VMEM((leaves + 2 * RIM + 1, num_vectors, points), BF16),
        pltpu.VMEM(leaf_basis.shape, BF16),
        pltpu.VMEM(near_blocks.shape, BF16),
        pltpu.VMEM(transfer_low.shape, BF16),
        pltpu.VMEM(coupling_low.shape, BF16),
        pltpu.VMEM(transfer_top.shape, BF16),
        pltpu.VMEM((top_used,) + coupling_top.shape[1:], BF16),
        pltpu.VMEM(vectors.shape, F32),
        pltpu.VMEM((coupling_low.shape[0], num_vectors, rank), F32),
        pltpu.VMEM((tree_devs + 1, num_vectors, 2 * rank), BF16),
        *boxes,
        pltpu.SemaphoreType.DMA((6 + top_used,)),
        pltpu.SemaphoreType.DMA((2 * low_levels,)),
        pltpu.SemaphoreType.DMA((2 * low_levels,)),
        pltpu.SemaphoreType.DMA,
        pltpu.SemaphoreType.DMA,
    ]
    sizes = (leaves, low_levels, tree_devs, num_sub, top_used, k_near, k_far)
    return pl.pallas_call(
        functools.partial(kernel, sizes),
        out_shape=jax.ShapeDtypeStruct(vectors.shape, BF16),
        in_specs=[pl.BlockSpec(memory_space=pltpu.SMEM)] * 4
        + [pl.BlockSpec(memory_space=pl.ANY)] * 7,
        out_specs=pl.BlockSpec(memory_space=pltpu.VMEM),
        scratch_shapes=scratch,
        compiler_params=pltpu.CompilerParams(
            collective_id=0, has_side_effects=True, vmem_limit_bytes=40 * 1024 * 1024
        ),
    )(
        near_list,
        near_mask,
        far_list,
        far_mask,
        vectors,
        leaf_basis,
        near_blocks,
        transfer_low,
        coupling_low,
        transfer_top,
        coupling_top,
    )


def solution(mesh):
    in_specs = (
        P(("copies", "leaf", "sub"), None, None),
        P(("copies", "leaf", "sub"), None, None),
        P(("copies", "leaf", "sub"), None, None, None),
        P(("leaf", "sub"), None),
        P(("leaf", "sub"), None),
        P(("copies", "leaf", "sub"), None, None),
        P(("copies", "leaf", "sub"), None, None, None),
        P(("leaf", "sub"), None),
        P(("leaf", "sub"), None),
        P("copies", None, None),
        P("copies", None, None, None),
    )
    out_specs = P(("copies", "leaf", "sub"), None, None)
    return jax.shard_map(
        per_device, mesh=mesh, in_specs=in_specs, out_specs=out_specs, check_vma=False
    )
```

time: 116 us -> 25.8 us (0.22)
  the two profiles are of different devices: /device:TPU:1 before, /device:TPU:0 now
where the time goes in v1:
time: 25.8 us; the launch traced here: 25.3 us
  Pallas kernels  13.4 us (52%)
  local copies, waits for them, and re-layouts  11.9 us (46%)
    pallas_call x1, Pallas kernels, per_device(): pl.pallas_call(functools.partial(kernel, sizes), out_shape=jax.ShapeDtype...  13.4 us
    unnamed x19, local copies, waits for them, and re-layouts  11.9 us

profile of v1, /device:TPU:0, one launch (start us, length us, event | category | flops | bytes accessed | tf_op | source)
XLA Modules:
  0.0 25.3 jit_solution(13967257408820344135)
XLA Ops:
  0.0 0.8 %copy.12.near_list = s32[16,6]{1,0:T(8,128)S(1)} copy(s32[16,6]{0,1:T(8,128)} %param.14) | data formatting | bytes 768 | tf_op args[3]
  0.8 0.8 %copy.13.near_mask = s32[16,6]{1,0:T(8,128)S(1)} copy(s32[16,6]{0,1:T(8,128)} %param.15) | data formatting | bytes 768 | tf_op args[4]
  1.5 0.8 %copy.14.far_list = s32[31,3]{1,0:T(8,128)S(1)} copy(s32[31,3]{0,1:T(4,128)} %param.18) | data formatting | bytes 744 | tf_op args[7]
  2.3 0.8 %copy.15.far_mask = s32[31,3]{1,0:T(8,128)S(1)} copy(s32[31,3]{0,1:T(4,128)} %param.19) | data formatting | bytes 744 | tf_op args[8]
  3.1 0.0 copy-start
  3.1 1.9 %copy-done = bf16[16,6,128,128]{3,2,1,0:T(8,128)(2,1)S(1)} copy-done((bf16[16,6,128,128]{3,2,1,0:T(8,128)(2,1)S(1)}, bf16[16,6,128,128]{3,2,1,0:T(8,128)(2,1)}, u32[]{:S(2)}) %copy-start) | copy-done | bytes 3145752
  5.0 0.0 copy-start.1
  5.0 1.4 %copy-done.1 = bf16[31,3,64,64]{3,2,1,0:T(8,128)(2,1)S(1)} copy-done((bf16[31,3,64,64]{3,2,1,0:T(8,128)(2,1)S(1)}, bf16[31,3,64,64]{3,2,1,0:T(8,128)(2,1)}, u32[]{:S(2)}) %copy-start.1) | copy-done | bytes 761880
  6.4 0.0 copy-start.2
  6.4 1.1 %copy-done.2 = bf16[14,3,64,64]{3,2,1,0:T(8,128)(2,1)S(1)} copy-done((bf16[14,3,64,64]{3,2,1,0:T(8,128)(2,1)S(1)}, bf16[14,3,64,64]{3,2,1,0:T(8,128)(2,1)}, u32[]{:S(2)}) %copy-start.2) | copy-done | bytes 344088
  7.5 0.0 copy-start.3
  7.5 1.0 %copy-done.3 = bf16[30,64,64]{2,1,0:T(8,128)(2,1)S(1)} copy-done((bf16[30,64,64]{2,1,0:T(8,128)(2,1)S(1)}, bf16[30,64,64]{2,1,0:T(8,128)(2,1)}, u32[]{:S(2)}) %copy-start.3) | copy-done | bytes 245784
  8.5 0.0 copy-start.4
  8.5 1.0 %copy-done.4 = bf16[30,64,64]{2,1,0:T(8,128)(2,1)S(1)} copy-done((bf16[30,64,64]{2,1,0:T(8,128)(2,1)S(1)}, bf16[30,64,64]{2,1,0:T(8,128)(2,1)}, u32[]{:S(2)}) %copy-start.4) | copy-done | bytes 245784
  9.5 0.0 copy-start.5
  9.5 0.9 %copy-done.5 = bf16[16,64,128]{2,1,0:T(8,128)(2,1)S(1)} copy-done((bf16[16,64,128]{2,1,0:T(8,128)(2,1)S(1)}, bf16[16,64,128]{2,1,0:T(8,128)(2,1)}, u32[]{:S(2)}) %copy-start.5) | copy-done | bytes 262168
  10.5 0.0 copy-start.6
  10.5 0.8 %copy-done.6 = bf16[16,16,128]{2,1,0:T(8,128)(2,1)S(1)} copy-done((bf16[16,16,128]{2,1,0:T(8,128)(2,1)S(1)}, bf16[16,16,128]{2,1,0:T(8,128)(2,1)}, u32[]{:S(2)}) %copy-start.6) | copy-done | bytes 65560
  11.3 13.4 %shard_map.109 = bf16[16,16,128]{2,1,0:T(8,128)(2,1)S(1)} custom-call(s32[16,6]{1,0:T(8,128)S(1)} %copy.12.near_list, s32[16,6]{1,0:T(8,128)S(1)} %copy.13.near_mask, s32[31,3]{1,0:T(8,128)S(1)} %copy.14.far_list, s32[31,3]{1,0:T(8,128)S(1)} %copy.15.far_mask, bf16[16,16,128]{2,1,0:T(8,128)(2,1)S(1)} %copy-done.6, bf16[16,64,128]{2,1,0:T(8,128)(2,1)S(1)} %copy-done.5, ...), custom_call_target="tpu_custom_call" | custom-call | tf_op jit(solution)/shard_map/pallas_call | solution.py:368
  24.7 0.6 %copy.17 = bf16[16,16,128]{2,1,0:T(8,128)(2,1)} copy(bf16[16,16,128]{2,1,0:T(8,128)(2,1)S(1)} %shard_map.109) | data formatting | bytes 131072
Async XLA Ops:
  3.1 1.9 %copy-start = (bf16[16,6,128,128]{3,2,1,0:T(8,128)(2,1)S(1)}, bf16[16,6,128,128]{3,2,1,0:T(8,128)(2,1)}, u32[]{:S(2)}) copy-start(bf16[16,6,128,128]{3,2,1,0:T(8,128)(2,1)} %near_blocks.1) | copy-start | bytes 9437188
  5.0 1.4 %copy-start.1 = (bf16[31,3,64,64]{3,2,1,0:T(8,128)(2,1)S(1)}, bf16[31,3,64,64]{3,2,1,0:T(8,128)(2,1)}, u32[]{:S(2)}) copy-start(bf16[31,3,64,64]{3,2,1,0:T(8,128)(2,1)} %coupling_low.1) | copy-start | bytes 2285572
  6.4 1.1 %copy-start.2 = (bf16[14,3,64,64]{3,2,1,0:T(8,128)(2,1)S(1)}, bf16[14,3,64,64]{3,2,1,0:T(8,128)(2,1)}, u32[]{:S(2)}) copy-start(bf16[14,3,64,64]{3,2,1,0:T(8,128)(2,1)} %coupling_top.1) | copy-start | bytes 1032196
  7.5 1.0 %copy-start.3 = (bf16[30,64,64]{2,1,0:T(8,128)(2,1)S(1)}, bf16[30,64,64]{2,1,0:T(8,128)(2,1)}, u32[]{:S(2)}) copy-start(bf16[30,64,64]{2,1,0:T(8,128)(2,1)} %transfer_low.1) | copy-start | bytes 737284
  8.5 1.0 %copy-start.4 = (bf16[30,64,64]{2,1,0:T(8,128)(2,1)S(1)}, bf16[30,64,64]{2,1,0:T(8,128)(2,1)}, u32[]{:S(2)}) copy-start(bf16[30,64,64]{2,1,0:T(8,128)(2,1)} %transfer_top.1) | copy-start | bytes 737284
  9.5 0.9 %copy-start.5 = (bf16[16,64,128]{2,1,0:T(8,128)(2,1)S(1)}, bf16[16,64,128]{2,1,0:T(8,128)(2,1)}, u32[]{:S(2)}) copy-start(bf16[16,64,128]{2,1,0:T(8,128)(2,1)} %basis.1) | copy-start | bytes 786436
  10.5 0.8 %copy-start.6 = (bf16[16,16,128]{2,1,0:T(8,128)(2,1)S(1)}, bf16[16,16,128]{2,1,0:T(8,128)(2,1)}, u32[]{:S(2)}) copy-start(bf16[16,16,128]{2,1,0:T(8,128)(2,1)} %vectors.1) | copy-start | bytes 196612

commit v2 on v1

--- a/solution.py
+++ b/solution.py
@@ -37,10 +37,10 @@
 
 def kernel(
     sizes,
-    near_list,
-    near_mask,
-    far_list,
-    far_mask,
+    near_list_in,
+    near_mask_in,
+    far_list_in,
+    far_mask_in,
     vectors,
     basis,
     near_blocks,
@@ -49,6 +49,10 @@
     transfer_top,
     coupling_top,
     out,
+    near_list,
+    near_mask,
+    far_list,
+    far_mask,
     vec_buf,
     basis_buf,
     near_buf,
@@ -86,7 +90,11 @@
         (vectors, vec_buf.at[pl.ds(RIM, leaves)]),
         (basis, basis_buf),
         (transfer_low, tlow_buf),
+        (near_list_in, near_list),
+        (near_mask_in, near_mask),
         (near_blocks, near_buf),
+        (far_list_in, far_list),
+        (far_mask_in, far_mask),
         (coupling_low, clow_buf),
         (transfer_top, ttop_buf),
     ]
@@ -194,15 +202,16 @@
     lax.fori_loop(1, tree_devs, send_root, 0, unroll=tree_devs <= 16)
 
     take_rims(0)
-    copies[3].wait()
+    for copy in copies[3:6]:
+        copy.wait()
     near_base = device * leaves - RIM
 
     def near_step(leaf, carry):
         sources = []
         for slot in range(k_near):
             spot = jnp.where(
-                near_mask[leaf, slot] != 0,
-                near_list[leaf, slot] - near_base,
+                near_mask[slot, leaf] != 0,
+                near_list[slot, leaf] - near_base,
                 leaves + 2 * RIM,
             )
             sources.append(vec_buf[spot])
@@ -216,7 +225,8 @@
 
     lax.fori_loop(0, leaves, near_step, 0, unroll=True)
 
-    copies[4].wait()
+    for copy in copies[6:9]:
+        copy.wait()
     for height in range(low_levels - 1):
         take_rims(height + 1)
         buf = level_bufs[height]
@@ -228,7 +238,7 @@
             total = None
             for slot in range(k_far):
                 spot = jnp.where(
-                    far_mask[row, slot] != 0, far_list[row, slot] - far_base, zero_spot
+                    far_mask[slot, row] != 0, far_list[slot, row] - far_base, zero_spot
                 )
                 term = jnp.dot(buf[spot], clow_buf[row, slot], preferred_element_type=F32)
                 total = term if total is None else total + term
@@ -237,7 +247,7 @@
 
         lax.fori_loop(0, counts[height], far_step, 0, unroll=True)
 
-    for copy in copies[5:]:
+    for copy in copies[9:]:
         copy.wait()
     arrived = roots.at[pl.ds(0, tree_devs - 1)]
     pltpu.make_async_copy(arrived, arrived, root_recv).wait()
@@ -264,7 +274,7 @@
         if height == 0:
             for slot in range(k_far):
                 spot = jnp.where(
-                    far_mask[root_row, slot] != 0, far_list[root_row, slot], tree_devs
+                    far_mask[slot, root_row] != 0, far_list[slot, root_row], tree_devs
                 )
                 term = jnp.dot(
                     roots[spot], doubled(clow_buf[root_row, slot]), preferred_element_type=F32
@@ -347,6 +357,10 @@
         for height in range(1, top_used + 1)
     ]
     scratch = [
+        pltpu.SMEM(near_list.shape[::-1], jnp.int32),
+        pltpu.SMEM(near_list.shape[::-1], jnp.int32),
+        pltpu.SMEM(far_list.shape[::-1], jnp.int32),
+        pltpu.SMEM(far_list.shape[::-1], jnp.int32),
         pltpu.VMEM((leaves + 2 * RIM + 1, num_vectors, points), BF16),
         pltpu.VMEM(leaf_basis.shape, BF16),
         pltpu.VMEM(near_blocks.shape, BF16),
@@ -358,7 +372,7 @@
         pltpu.VMEM((coupling_low.shape[0], num_vectors, rank), F32),
         pltpu.VMEM((tree_devs + 1, num_vectors, 2 * rank), BF16),
         *boxes,
-        pltpu.SemaphoreType.DMA((6 + top_used,)),
+        pltpu.SemaphoreType.DMA((10 + top_used,)),
         pltpu.SemaphoreType.DMA((2 * low_levels,)),
         pltpu.SemaphoreType.DMA((2 * low_levels,)),
         pltpu.SemaphoreType.DMA,
@@ -368,18 +382,17 @@
     return pl.pallas_call(
         functools.partial(kernel, sizes),
         out_shape=jax.ShapeDtypeStruct(vectors.shape, BF16),
-        in_specs=[pl.BlockSpec(memory_space=pltpu.SMEM)] * 4
-        + [pl.BlockSpec(memory_space=pl.ANY)] * 7,
+        in_specs=[pl.BlockSpec(memory_space=pltpu.HBM)] * 11,
         out_specs=pl.BlockSpec(memory_space=pltpu.VMEM),
         scratch_shapes=scratch,
         compiler_params=pltpu.CompilerParams(
-            collective_id=0, has_side_effects=True, vmem_limit_bytes=40 * 1024 * 1024
+            collective_id=0, has_side_effects=True, vmem_limit_bytes=60 * 1024 * 1024
         ),
     )(
-        near_list,
-        near_mask,
-        far_list,
-        far_mask,
+        near_list.T,
+        near_mask.T,
+        far_list.T,
+        far_mask.T,
         vectors,
         leaf_basis,
         near_blocks,

time: 25.8 us -> 14 us (0.54); the launches traced: 25.3 us -> 13.9 us
  local copies, waits for them, and re-layouts: 11.9 us -> 1.47 us
  Pallas kernels: 13.4 us -> 12.4 us
    unnamed x19 -> x1, local copies, waits for them, and re-layouts: 11.9 us -> 1.47 us
    pallas_call x1, Pallas kernels: 13.4 us -> 12.4 us  [per_device(): pl.pallas_call(functools.partial(kernel, sizes), out_shape=jax.ShapeDtype...]
where the time goes in v2:
time: 14 us; the launch traced here: 13.9 us
  Pallas kernels  12.4 us (89%)
  local copies, waits for them, and re-layouts  1.47 us (10%)
    pallas_call x1, Pallas kernels, per_device(): pl.pallas_call(functools.partial(kernel, sizes), out_shape=jax.ShapeDtype...  12.4 us
    unnamed x1, local copies, waits for them, and re-layouts  1.47 us

profile of v2, /device:TPU:0, one launch (start us, length us, event | category | flops | bytes accessed | tf_op | source)
XLA Modules:
  0.0 13.9 jit_solution(5403488322174473068)
XLA Ops:
  0.0 12.4 %shard_map.109 = bf16[16,16,128]{2,1,0:T(8,128)(2,1)} custom-call(s32[6,16]{1,0:T(8,128)} %bitcast.4, s32[6,16]{1,0:T(8,128)} %bitcast.5, s32[3,31]{1,0:T(4,128)} %bitcast.6, s32[3,31]{1,0:T(4,128)} %bitcast.7, bf16[16,16,128]{2,1,0:T(8,128)(2,1)} %vectors.1, bf16[16,64,128]{2,1,0:T(8,128)(2,1)} %basis.1, bf16[16,6,128,128]{3,2,1,0:T(8,128)(2,1)} %near_blocks.1, ...), custom_call_target="tpu_custom_call" | custom-call | tf_op jit(solution)/shard_map/pallas_call | solution.py:382
  12.4 1.5 %copy.13 = bf16[16,16,128]{2,1,0:T(8,128)(2,1)} copy(bf16[16,16,128]{2,1,0:T(8,128)(2,1)} %shard_map.109) | data formatting | bytes 131072

commit v3 on v2

--- a/solution.py
+++ b/solution.py
@@ -84,8 +84,6 @@
         )
         return carry
 
-    lax.fori_loop(1, tree_devs, greet, 0, unroll=tree_devs <= 16)
-
     moves = [
         (vectors, vec_buf.at[pl.ds(RIM, leaves)]),
         (basis, basis_buf),
@@ -105,7 +103,10 @@
         pltpu.make_async_copy(source, target, local_sem.at[at])
         for at, (source, target) in enumerate(moves)
     ]
-    for copy in copies:
+    for copy in copies[:3]:
+        copy.start()
+    lax.fori_loop(1, tree_devs, greet, 0, unroll=tree_devs <= 16)
+    for copy in copies[3:]:
         copy.start()
 
     starts = [2 * leaves - 2 * (leaves >> height) for height in range(low_levels)]
@@ -172,9 +173,6 @@
     coefs = bdot(vec_buf[pl.ds(RIM, leaves)], basis_buf[...], transposed=True)
     pieces = stacked(coefs)
     level_bufs[0][pl.ds(rims[0], counts[0])] = pieces
-    pl.semaphore_wait(barrier, tree_devs - 1)
-    send_rims(0)
-    send_rims(1)
     copies[2].wait()
     for height in range(1, low_levels):
         below = counts[height - 1]
@@ -184,9 +182,10 @@
         if height < low_levels - 1:
             pieces = stacked(coefs)
             level_bufs[height][pl.ds(rims[height], counts[height])] = pieces
-            send_rims(height + 1)
     high, low = split(coefs[0])
     roots[device] = jnp.concatenate([high.astype(F32), low.astype(F32)], axis=-1).astype(BF16)
+
+    pl.semaphore_wait(barrier, tree_devs - 1)
 
     def send_root(step, carry):
         pltpu.make_async_remote_copy(
@@ -200,6 +199,8 @@
         return carry
 
     lax.fori_loop(1, tree_devs, send_root, 0, unroll=tree_devs <= 16)
+    for at in range(low_levels):
+        send_rims(at)
 
     take_rims(0)
     for copy in copies[3:6]:
@@ -381,7 +382,7 @@
     sizes = (leaves, low_levels, tree_devs, num_sub, top_used, k_near, k_far)
     return pl.pallas_call(
         functools.partial(kernel, sizes),
-        out_shape=jax.ShapeDtypeStruct(vectors.shape, BF16),
+        out_shape=pltpu.VMEM(vectors.shape, BF16),
         in_specs=[pl.BlockSpec(memory_space=pltpu.HBM)] * 11,
         out_specs=pl.BlockSpec(memory_space=pltpu.VMEM),
         scratch_shapes=scratch,

time: 14 us -> 12.1 us (0.86)
  the two profiles are of different devices: /device:TPU:0 before, /device:TPU:1 now
where the time goes in v3:
time: 12.1 us; the launch traced here: 11.9 us
  Pallas kernels  11.3 us (93%)
  local copies, waits for them, and re-layouts  0.63 us (5%)
    pallas_call x1, Pallas kernels, per_device(): pl.pallas_call(functools.partial(kernel, sizes), out_shape=pltpu.VMEM(vec...  11.3 us
    unnamed x1, local copies, waits for them, and re-layouts  0.63 us

profile of v3, /device:TPU:1, one launch (start us, length us, event | category | flops | bytes accessed | tf_op | source)
XLA Modules:
  0.0 11.9 jit_solution(1483063626366512239)
XLA Ops:
  0.0 11.3 %shard_map.109 = bf16[16,16,128]{2,1,0:T(8,128)(2,1)S(1)} custom-call(s32[6,16]{1,0:T(8,128)} %bitcast.4, s32[6,16]{1,0:T(8,128)} %bitcast.5, s32[3,31]{1,0:T(4,128)} %bitcast.6, s32[3,31]{1,0:T(4,128)} %bitcast.7, bf16[16,16,128]{2,1,0:T(8,128)(2,1)} %vectors.1, bf16[16,64,128]{2,1,0:T(8,128)(2,1)} %basis.1, bf16[16,6,128,128]{3,2,1,0:T(8,128)(2,1)} %near_blocks.1, ...), custom_call_target="tpu_custom_call" | custom-call | tf_op jit(solution)/shard_map/pallas_call | solution.py:383
  11.3 0.6 %copy.13 = bf16[16,16,128]{2,1,0:T(8,128)(2,1)} copy(bf16[16,16,128]{2,1,0:T(8,128)(2,1)S(1)} %shard_map.109) | data formatting | bytes 131072

commit v4 on v3

v4 whole, which is shorter than its diff:
```python
import functools

import jax
import jax.numpy as jnp
from jax import lax
from jax.experimental import pallas as pl
from jax.experimental.pallas import tpu as pltpu
from jax.sharding import PartitionSpec as P

RIM = 2
MESH = pl.DeviceIdType.MESH
F32 = jnp.float32
BF16 = jnp.bfloat16


def bdot(left, right, transposed=False):
    contract = 2 if transposed else 1
    return lax.dot_general(
        left, right, (((2,), (contract,)), ((0,), (0,))), preferred_element_type=F32
    )


def split(value):
    high = value.astype(BF16)
    low = (value - high.astype(F32)).astype(BF16)
    return high, low


def stacked(value):
    return jnp.concatenate(split(value), axis=-2)


def folded(value):
    half = value.shape[-2] // 2
    return value[..., :half, :] + value[..., half:, :]


def packed(value):
    high = value.astype(BF16).astype(F32)
    return jnp.concatenate([high, value - high], axis=-1).astype(BF16)


def doubled(matrix):
    return jnp.concatenate([matrix, matrix], axis=-2)


def dot(left, right, transposed=False):
    contract = 1 if transposed else 0
    return lax.dot_general(
        left, right, (((1,), (contract,)), ((), ())), preferred_element_type=F32
    )


def kernel(
    sizes,
    near_list_in,
    near_mask_in,
    far_list_in,
    far_mask_in,
    vectors,
    basis,
    near_blocks,
    transfer_low,
    coupling_low,
    transfer_top,
    coupling_top,
    out,
    near_list,
    near_mask,
    far_list,
    far_mask,
    vec_buf,
    basis_buf,
    near_buf,
    tlow_buf,
    clow_buf,
    ttop_buf,
    ctop_buf,
    near_acc,
    far_acc,
    roots,
    *rest,
):
    leaves, low_levels, tree_devs, num_sub, top_used, k_near, k_far = sizes
    level_bufs = rest[: low_levels - 1]
    rim_out, rim_in, path_buf, leaf_ways = rest[low_levels - 1 : -5]
    local_sem, rim_send, rim_recv, root_send, root_recv = rest[-5:]
    leaf_at = lax.axis_index("leaf")
    device = leaf_at * num_sub + lax.axis_index("sub")
    copy_at = lax.axis_index("copies")

    def place(index):
        return (copy_at, index // num_sub, index % num_sub)

    barrier = pltpu.get_barrier_semaphore()

    def greet(step, carry):
        pl.semaphore_signal(
            barrier, inc=1, device_id=place((device + step) % tree_devs), device_id_type=MESH
        )
        return carry

    moves = [
        (vectors, vec_buf.at[pl.ds(RIM, leaves)]),
        (basis, basis_buf),
        (transfer_low, tlow_buf),
        (near_list_in, near_list),
        (near_mask_in, near_mask),
        (near_blocks, near_buf),
        (far_list_in, far_list),
        (far_mask_in, far_mask),
        (coupling_low, clow_buf),
        (transfer_top, ttop_buf),
    ]
    for height in range(1, top_used + 1):
        row = tree_devs - 2 * (tree_devs >> height) + device // (1 << height)
        moves.append((coupling_top.at[row], ctop_buf.at[height - 1]))
    copies = [
        pltpu.make_async_copy(source, target, local_sem.at[at])
        for at, (source, target) in enumerate(moves)
    ]
    for copy in copies[:3]:
        copy.start()
    lax.fori_loop(1, tree_devs, greet, 0, unroll=tree_devs <= 16)
    for copy in copies[3:]:
        copy.start()

    starts = [2 * leaves - 2 * (leaves >> height) for height in range(low_levels)]
    counts = [leaves >> height for height in range(low_levels)]
    rims = [min(RIM, count) for count in counts]

    vec_buf[leaves + 2 * RIM] = jnp.zeros(vec_buf.shape[1:], BF16)
    for buf in level_bufs:
        buf[buf.shape[0] - 1] = jnp.zeros(buf.shape[1:], BF16)
    roots[tree_devs] = jnp.zeros(roots.shape[1:], BF16)

    parts = [(vec_buf, leaves, RIM)]
    parts += [(level_bufs[height], counts[height], rims[height]) for height in range(low_levels - 1)]

    to_right, to_left = [
        pltpu.make_async_remote_copy(
            src_ref=rim_out.at[side],
            dst_ref=rim_in.at[side],
            send_sem=rim_send.at[side],
            recv_sem=rim_recv.at[side],
            device_id=place(device + step),
            device_id_type=MESH,
        )
        for side, step in ((0, 1), (1, -1))
    ]
    has_right = device < tree_devs - 1
    has_left = device > 0

    copies[0].wait()
    copies[1].wait()
    coefs = bdot(vec_buf[pl.ds(RIM, leaves)], basis_buf[...], transposed=True)
    level_coefs = [coefs]
    copies[2].wait()
    for height in range(1, low_levels):
        below = counts[height - 1]
        moved = folded(bdot(stacked(coefs), tlow_buf[pl.ds(starts[height - 1], below)]))
        moved = moved.reshape((below // 2, 2) + moved.shape[1:])
        coefs = moved[:, 0] + moved[:, 1]
        level_coefs.append(coefs)
    roots[device] = packed(coefs[0])
    pl.semaphore_wait(barrier, tree_devs - 1)

    def send_root(step, carry):
        pltpu.make_async_remote_copy(
            src_ref=roots.at[device],
            dst_ref=roots.at[device],
            send_sem=root_send,
            recv_sem=root_recv,
            device_id=place((device + step) % tree_devs),
            device_id_type=MESH,
        ).start()
        return carry

    lax.fori_loop(1, tree_devs, send_root, 0, unroll=tree_devs <= 16)

    for height in range(low_levels - 1):
        level_bufs[height][pl.ds(rims[height], counts[height])] = packed(level_coefs[height])
    at = 0
    for buf, count, rim in parts:
        rim_out[0, pl.ds(at, rim)] = buf[pl.ds(count, rim)]
        rim_out[1, pl.ds(at, rim)] = buf[pl.ds(rim, rim)]
        at += rim

    @pl.when(has_right)
    def _():
        to_right.start()

    @pl.when(has_left)
    def _():
        to_left.start()

    for copy in copies[3:]:
        copy.wait()

    def first_of(height):
        return 2 * tree_devs - 2 * (tree_devs >> height)

    sources = []
    root_row = starts[low_levels - 1]
    for slot in range(k_far):
        spot = jnp.where(far_mask[slot, root_row] != 0, far_list[slot, root_row], tree_devs)
        path_buf[len(sources)] = packed(clow_buf[root_row, slot].astype(F32))
        sources.append(spot)

    def expand(height, box, inside, matrix):
        if height == 0:
            path_buf[len(sources)] = packed(matrix)
            sources.append(jnp.where(inside, box, tree_devs))
            return
        mats = ttop_buf[pl.ds(first_of(height - 1) + 2 * box, 2)]
        mats = mats.reshape(2 * mats.shape[1], mats.shape[2])
        high, low = split(matrix)
        both = dot(mats, high) + dot(mats, low)
        rank = matrix.shape[0]
        expand(height - 1, 2 * box, inside, both[:rank])
        expand(height - 1, 2 * box + 1, inside, both[rank:])

    for height in range(1, top_used + 1):
        node = device // (1 << height)
        boxes = tree_devs >> height
        chain = ctop_buf[height - 1]
        rank = chain.shape[1]
        chain = chain.reshape(chain.shape[0] * rank, chain.shape[2])
        for step in range(height - 1, -1, -1):
            matrix = ttop_buf[first_of(step) + device // (1 << step)]
            if step == height - 1:
                chain = dot(chain, matrix, transposed=True)
            else:
                chain = folded(dot(stacked(chain), matrix, transposed=True))
        odd = node % 2
        for slot, (even_step, odd_step) in enumerate(((-2, -3), (2, -2), (3, 2))):
            box = node + jnp.where(odd == 1, odd_step, even_step)
            inside = (box >= 0) & (box < boxes)
            box = jnp.where(inside, box, 0)
            expand(height, box, inside, chain[slot * rank : (slot + 1) * rank])

    rank = tlow_buf.shape[1]
    rows = lax.broadcasted_iota(jnp.int32, (rank, rank), 0)
    columns = lax.broadcasted_iota(jnp.int32, (rank, rank), 1)
    unit = jnp.where(rows == columns, 1.0, 0.0).astype(BF16)
    ways = [unit]
    for height in range(low_levels - 2, -1, -1):
        following = []
        for box in range(counts[height]):
            way = ways[box // 2]
            moved = dot(way, tlow_buf[starts[height] + box], transposed=True)
            if height == low_levels - 2:
                moved = moved.astype(BF16)
            else:
                moved = stacked(moved if way.shape[0] == rank else folded(moved))
            following.append(moved)
        ways = following
    for leaf in range(leaves):
        moved = dot(ways[leaf], basis_buf[leaf])
        leaf_ways[leaf] = stacked(moved if ways[leaf].shape[0] == rank else folded(moved))

    @pl.when(has_left)
    def _():
        to_right.wait_recv()

    @pl.when(has_right)
    def _():
        to_left.wait_recv()

    at = 0
    for buf, count, rim in parts:
        buf[pl.ds(0, rim)] = rim_in[0, pl.ds(at, rim)]
        buf[pl.ds(rim + count, rim)] = rim_in[1, pl.ds(at, rim)]
        at += rim

    near_base = device * leaves - RIM

    def near_step(leaf, carry):
        beside = []
        for slot in range(k_near):
            spot = jnp.where(
                near_mask[slot, leaf] != 0,
                near_list[slot, leaf] - near_base,
                leaves + 2 * RIM,
            )
            beside.append(vec_buf[spot])
        blocks = near_buf[leaf]
        near_acc[leaf] = dot(
            jnp.concatenate(beside, axis=-1),
            blocks.reshape(blocks.shape[0] * blocks.shape[1], blocks.shape[2]),
        )
        return carry

    lax.fori_loop(0, leaves, near_step, 0, unroll=True)

    for height in range(low_levels - 1):
        buf = level_bufs[height]
        far_base = device * counts[height] - rims[height]
        zero_spot = buf.shape[0] - 1

        def far_step(box, carry, buf=buf, far_base=far_base, zero_spot=zero_spot, height=height):
            row = starts[height] + box
            total = None
            for slot in range(k_far):
                spot = jnp.where(
                    far_mask[slot, row] != 0, far_list[slot, row] - far_base, zero_spot
                )
                term = dot(buf[spot], doubled(clow_buf[row, slot]))
                total = term if total is None else total + term
            far_acc[row] = total
            return carry

        lax.fori_loop(0, counts[height], far_step, 0, unroll=True)

    expanded = None
    for height in range(low_levels - 2, -1, -1):
        count = counts[height]
        own = far_acc[pl.ds(starts[height], count)]
        if expanded is not None:
            spread = stacked(expanded)
            spread = jnp.broadcast_to(spread[:, None], (count // 2, 2) + spread.shape[1:])
            spread = spread.reshape((count,) + spread.shape[2:])
            mats = tlow_buf[pl.ds(starts[height], count)]
            own = own + folded(bdot(spread, mats, transposed=True))
        expanded = own
    near_acc[...] = near_acc[...] + folded(bdot(stacked(expanded), basis_buf[...]))

    arrived = roots.at[pl.ds(0, tree_devs - 1)]
    pltpu.make_async_copy(arrived, arrived, root_recv).wait()
    total = None
    for at, spot in enumerate(sources):
        term = dot(roots[spot], doubled(path_buf[at]))
        total = term if total is None else total + term
    downward = stacked(total + pltpu.roll(total, rank, 1))
    for leaf in range(leaves):
        out[leaf] = (near_acc[leaf] + folded(dot(downward, leaf_ways[leaf]))).astype(out.dtype)

    sent = roots.at[pl.ds(0, tree_devs - 1)]
    pltpu.make_async_copy(sent, sent, root_send).wait()

    @pl.when(has_right)
    def _():
        to_right.wait_send()

    @pl.when(has_left)
    def _():
        to_left.wait_send()


def per_device(
    vectors,
    leaf_basis,
    near_blocks,
    near_list,
    near_mask,
    transfer_low,
    coupling_low,
    far_list,
    far_mask,
    transfer_top,
    coupling_top,
):
    tree_devs = lax.axis_size(("leaf", "sub"))
    num_sub = lax.axis_size("sub")
    leaves, num_vectors, points = vectors.shape
    rank = leaf_basis.shape[1]
    k_near = near_blocks.shape[1]
    k_far = coupling_low.shape[1]
    low_levels = leaves.bit_length()
    top_used = max(tree_devs.bit_length() - 3, 0)
    counts = [leaves >> height for height in range(low_levels - 1)]
    boxes = [
        pltpu.VMEM((count + 2 * min(RIM, count) + 1, num_vectors, 2 * rank), BF16)
        for count in counts
    ]
    rim_boxes = RIM + sum(min(RIM, count) for count in counts)
    paths = k_far * sum(1 << height for height in range(top_used + 1))
    scratch = [
        pltpu.SMEM(near_list.shape[::-1], jnp.int32),
        pltpu.SMEM(near_list.shape[::-1], jnp.int32),
        pltpu.SMEM(far_list.shape[::-1], jnp.int32),
        pltpu.SMEM(far_list.shape[::-1], jnp.int32),
        pltpu.VMEM((leaves + 2 * RIM + 1, num_vectors, points), BF16),
        pltpu.VMEM(leaf_basis.shape, BF16),
        pltpu.VMEM(near_blocks.shape, BF16),
        pltpu.VMEM(transfer_low.shape, BF16),
        pltpu.VMEM(coupling_low.shape, BF16),
        pltpu.VMEM(transfer_top.shape, BF16),
        pltpu.VMEM((top_used,) + coupling_top.shape[1:], BF16),
        pltpu.VMEM(vectors.shape, F32),
        pltpu.VMEM((coupling_low.shape[0], num_vectors, rank), F32),
        pltpu.VMEM((tree_devs + 1, num_vectors, 2 * rank), BF16),
        *boxes,
        pltpu.VMEM((2, rim_boxes, num_vectors, points), BF16),
        pltpu.VMEM((2, rim_boxes, num_vectors, points), BF16),
        pltpu.VMEM((paths, rank, 2 * rank), BF16),
        pltpu.VMEM((leaves, 2 * rank, points), BF16),
        pltpu.SemaphoreType.DMA((10 + top_used,)),
        pltpu.SemaphoreType.DMA((2,)),
        pltpu.SemaphoreType.DMA((2,)),
        pltpu.SemaphoreType.DMA,
        pltpu.SemaphoreType.DMA,
    ]
    sizes = (leaves, low_levels, tree_devs, num_sub, top_used, k_near, k_far)
    return pl.pallas_call(
        functools.partial(kernel, sizes),
        out_shape=pltpu.VMEM(vectors.shape, BF16),
        in_specs=[pl.BlockSpec(memory_space=pltpu.HBM)] * 11,
        out_specs=pl.BlockSpec(memory_space=pltpu.VMEM),
        scratch_shapes=scratch,
        compiler_params=pltpu.CompilerParams(
            collective_id=0, has_side_effects=True, vmem_limit_bytes=60 * 1024 * 1024
        ),
    )(
        near_list.T,
        near_mask.T,
        far_list.T,
        far_mask.T,
        vectors,
        leaf_basis,
        near_blocks,
        transfer_low,
        coupling_low,
        transfer_top,
        coupling_top,
    )


def solution(mesh):
    in_specs = (
        P(("copies", "leaf", "sub"), None, None),
        P(("copies", "leaf", "sub"), None, None),
        P(("copies", "leaf", "sub"), None, None, None),
        P(("leaf", "sub"), None),
        P(("leaf", "sub"), None),
        P(("copies", "leaf", "sub"), None, None),
        P(("copies", "leaf", "sub"), None, None, None),
        P(("leaf", "sub"), None),
        P(("leaf", "sub"), None),
        P("copies", None, None),
        P("copies", None, None, None),
    )
    out_specs = P(("copies", "leaf", "sub"), None, None)
    return jax.shard_map(
        per_device, mesh=mesh, in_specs=in_specs, out_specs=out_specs, check_vma=False
    )
```

time: 12.1 us -> 12.4 us (1.025)
  Pallas kernels: 11.3 us -> 11.6 us
    pallas_call x1, Pallas kernels: 11.3 us -> 11.6 us  [per_device(): pl.pallas_call(functools.partial(kernel, sizes), out_shape=pltpu.VMEM(vec...]
where the time goes in v4:
time: 12.4 us; the launch traced here: 12.3 us
  Pallas kernels  11.6 us (94%)
  local copies, waits for them, and re-layouts  0.63 us (5%)
    pallas_call x1, Pallas kernels, per_device(): pl.pallas_call(functools.partial(kernel, sizes), out_shape=pltpu.VMEM(vec...  11.6 us
    unnamed x1, local copies, waits for them, and re-layouts  0.63 us

profile of v4, /device:TPU:1, one launch (start us, length us, event | category | flops | bytes accessed | tf_op | source)
XLA Modules:
  0.0 12.3 jit_solution(7292261824046217735)
XLA Ops:
  0.0 11.6 %shard_map.109 = bf16[16,16,128]{2,1,0:T(8,128)(2,1)S(1)} custom-call(s32[6,16]{1,0:T(8,128)} %bitcast.4, s32[6,16]{1,0:T(8,128)} %bitcast.5, s32[3,31]{1,0:T(4,128)} %bitcast.6, s32[3,31]{1,0:T(4,128)} %bitcast.7, bf16[16,16,128]{2,1,0:T(8,128)(2,1)} %vectors.1, bf16[16,64,128]{2,1,0:T(8,128)(2,1)} %basis.1, bf16[16,6,128,128]{3,2,1,0:T(8,128)(2,1)} %near_blocks.1, ...), custom_call_target="tpu_custom_call" | custom-call | tf_op jit(solution)/shard_map/pallas_call | solution.py:405
  11.7 0.6 %copy.13 = bf16[16,16,128]{2,1,0:T(8,128)(2,1)} copy(bf16[16,16,128]{2,1,0:T(8,128)(2,1)S(1)} %shard_map.109) | data formatting | bytes 131072

commit v5 on v4

--- a/solution.py
+++ b/solution.py
@@ -38,6 +38,21 @@
 def packed(value):
     high = value.astype(BF16).astype(F32)
     return jnp.concatenate([high, value - high], axis=-1).astype(BF16)
+
+
+def packed_twin(value):
+    high = value.astype(BF16).astype(F32)
+    lanes = lax.broadcasted_iota(jnp.int32, value.shape, value.ndim - 1)
+    return jnp.where(lanes < value.shape[-1] // 2, high, value - high).astype(BF16)
+
+
+def unpacked(pair):
+    rank = pair.shape[-1] // 2
+    return jnp.concatenate([pair[..., :rank], pair[..., rank:]], axis=-2)
+
+
+def twin(value):
+    return value + pltpu.roll(value, value.shape[-1] // 2, value.ndim - 1)
 
 
 def doubled(matrix):
@@ -134,9 +149,6 @@
         buf[buf.shape[0] - 1] = jnp.zeros(buf.shape[1:], BF16)
     roots[tree_devs] = jnp.zeros(roots.shape[1:], BF16)
 
-    parts = [(vec_buf, leaves, RIM)]
-    parts += [(level_bufs[height], counts[height], rims[height]) for height in range(low_levels - 1)]
-
     to_right, to_left = [
         pltpu.make_async_remote_copy(
             src_ref=rim_out.at[side],
@@ -155,10 +167,12 @@
     copies[1].wait()
     coefs = bdot(vec_buf[pl.ds(RIM, leaves)], basis_buf[...], transposed=True)
     level_coefs = [coefs]
+    pieces = []
     copies[2].wait()
     for height in range(1, low_levels):
         below = counts[height - 1]
-        moved = folded(bdot(stacked(coefs), tlow_buf[pl.ds(starts[height - 1], below)]))
+        pieces.append(stacked(coefs))
+        moved = folded(bdot(pieces[-1], tlow_buf[pl.ds(starts[height - 1], below)]))
         moved = moved.reshape((below // 2, 2) + moved.shape[1:])
         coefs = moved[:, 0] + moved[:, 1]
         level_coefs.append(coefs)
@@ -178,22 +192,24 @@
 
     lax.fori_loop(1, tree_devs, send_root, 0, unroll=tree_devs <= 16)
 
+    rim_out[0, pl.ds(0, RIM)] = vec_buf[pl.ds(leaves, RIM)]
+    rim_out[1, pl.ds(0, RIM)] = vec_buf[pl.ds(RIM, RIM)]
+    at = RIM
+    for count, rim, coefs in zip(counts, rims, level_coefs[:-1]):
+        rim_out[0, pl.ds(at, rim)] = packed(coefs[count - rim :])
+        rim_out[1, pl.ds(at, rim)] = packed(coefs[:rim])
+        at += rim
+
+    @pl.when(has_right)
+    def _():
+        to_right.start()
+
+    @pl.when(has_left)
+    def _():
+        to_left.start()
+
     for height in range(low_levels - 1):
-        level_bufs[height][pl.ds(rims[height], counts[height])] = packed(level_coefs[height])
-    at = 0
-    for buf, count, rim in parts:
-        rim_out[0, pl.ds(at, rim)] = buf[pl.ds(count, rim)]
-        rim_out[1, pl.ds(at, rim)] = buf[pl.ds(rim, rim)]
-        at += rim
-
-    @pl.when(has_right)
-    def _():
-        to_right.start()
-
-    @pl.when(has_left)
-    def _():
-        to_left.start()
-
+        level_bufs[height][pl.ds(rims[height], counts[height])] = pieces[height]
     for copy in copies[3:]:
         copy.wait()
 
@@ -204,18 +220,19 @@
     root_row = starts[low_levels - 1]
     for slot in range(k_far):
         spot = jnp.where(far_mask[slot, root_row] != 0, far_list[slot, root_row], tree_devs)
-        path_buf[len(sources)] = packed(clow_buf[root_row, slot].astype(F32))
+        near_path = clow_buf[root_row, slot]
+        path_buf[len(sources)] = jnp.concatenate([near_path, jnp.zeros_like(near_path)], axis=-1)
         sources.append(spot)
 
     def expand(height, box, inside, matrix):
+        matrix = packed_twin(matrix)
         if height == 0:
-            path_buf[len(sources)] = packed(matrix)
+            path_buf[len(sources)] = matrix
             sources.append(jnp.where(inside, box, tree_devs))
             return
         mats = ttop_buf[pl.ds(first_of(height - 1) + 2 * box, 2)]
         mats = mats.reshape(2 * mats.shape[1], mats.shape[2])
-        high, low = split(matrix)
-        both = dot(mats, high) + dot(mats, low)
+        both = twin(dot(mats, matrix))
         rank = matrix.shape[0]
         expand(height - 1, 2 * box, inside, both[:rank])
         expand(height - 1, 2 * box + 1, inside, both[rank:])
@@ -228,6 +245,8 @@
         chain = chain.reshape(chain.shape[0] * rank, chain.shape[2])
         for step in range(height - 1, -1, -1):
             matrix = ttop_buf[first_of(step) + device // (1 << step)]
+            if step == 0:
+                matrix = doubled(matrix)
             if step == height - 1:
                 chain = dot(chain, matrix, transposed=True)
             else:
@@ -267,10 +286,12 @@
     def _():
         to_left.wait_recv()
 
-    at = 0
-    for buf, count, rim in parts:
-        buf[pl.ds(0, rim)] = rim_in[0, pl.ds(at, rim)]
-        buf[pl.ds(rim + count, rim)] = rim_in[1, pl.ds(at, rim)]
+    vec_buf[pl.ds(0, RIM)] = rim_in[0, pl.ds(0, RIM)]
+    vec_buf[pl.ds(RIM + leaves, RIM)] = rim_in[1, pl.ds(0, RIM)]
+    at = RIM
+    for buf, count, rim in zip(level_bufs, counts, rims):
+        buf[pl.ds(0, rim)] = unpacked(rim_in[0, pl.ds(at, rim)])
+        buf[pl.ds(rim + count, rim)] = unpacked(rim_in[1, pl.ds(at, rim)])
         at += rim
 
     near_base = device * leaves - RIM
@@ -305,9 +326,9 @@
                 spot = jnp.where(
                     far_mask[slot, row] != 0, far_list[slot, row] - far_base, zero_spot
                 )
-                term = dot(buf[spot], doubled(clow_buf[row, slot]))
+                term = dot(buf[spot], clow_buf[row, slot])
                 total = term if total is None else total + term
-            far_acc[row] = total
+            far_acc[row] = folded(total)
             return carry
 
         lax.fori_loop(0, counts[height], far_step, 0, unroll=True)
@@ -328,10 +349,14 @@
     arrived = roots.at[pl.ds(0, tree_devs - 1)]
     pltpu.make_async_copy(arrived, arrived, root_recv).wait()
     total = None
-    for at, spot in enumerate(sources):
-        term = dot(roots[spot], doubled(path_buf[at]))
+    for first in range(0, len(sources), 8):
+        group = range(first, min(first + 8, len(sources)))
+        term = dot(
+            jnp.concatenate([roots[sources[at]] for at in group], axis=-1),
+            jnp.concatenate([doubled(path_buf[at]) for at in group], axis=-2),
+        )
         total = term if total is None else total + term
-    downward = stacked(total + pltpu.roll(total, rank, 1))
+    downward = stacked(twin(total))
     for leaf in range(leaves):
         out[leaf] = (near_acc[leaf] + folded(dot(downward, leaf_ways[leaf]))).astype(out.dtype)
 
@@ -370,7 +395,7 @@
     top_used = max(tree_devs.bit_length() - 3, 0)
     counts = [leaves >> height for height in range(low_levels - 1)]
     boxes = [
-        pltpu.VMEM((count + 2 * min(RIM, count) + 1, num_vectors, 2 * rank), BF16)
+        pltpu.VMEM((count + 2 * min(RIM, count) + 1, 2 * num_vectors, rank), BF16)
         for count in counts
     ]
     rim_boxes = RIM + sum(min(RIM, count) for count in counts)

time: 12.4 us -> 11.7 us (0.944)
  Pallas kernels: 11.6 us -> 10.9 us
    pallas_call x1, Pallas kernels: 11.6 us -> 10.9 us  [per_device(): pl.pallas_call(functools.partial(kernel, sizes), out_shape=pltpu.VMEM(vec...]
where the time goes in v5:
time: 11.7 us; the launch traced here: 11.5 us
  Pallas kernels  10.9 us (93%)
  local copies, waits for them, and re-layouts  0.63 us (5%)
    pallas_call x1, Pallas kernels, per_device(): pl.pallas_call(functools.partial(kernel, sizes), out_shape=pltpu.VMEM(vec...  10.9 us
    unnamed x1, local copies, waits for them, and re-layouts  0.63 us

profile of v5, /device:TPU:1, one launch (start us, length us, event | category | flops | bytes accessed | tf_op | source)
XLA Modules:
  0.0 11.5 jit_solution(16802794695560064116)
XLA Ops:
  0.0 10.9 %shard_map.109 = bf16[16,16,128]{2,1,0:T(8,128)(2,1)S(1)} custom-call(s32[6,16]{1,0:T(8,128)} %bitcast.4, s32[6,16]{1,0:T(8,128)} %bitcast.5, s32[3,31]{1,0:T(4,128)} %bitcast.6, s32[3,31]{1,0:T(4,128)} %bitcast.7, bf16[16,16,128]{2,1,0:T(8,128)(2,1)} %vectors.1, bf16[16,64,128]{2,1,0:T(8,128)(2,1)} %basis.1, bf16[16,6,128,128]{3,2,1,0:T(8,128)(2,1)} %near_blocks.1, ...), custom_call_target="tpu_custom_call" | custom-call | tf_op jit(solution)/shard_map/pallas_call | solution.py:430
  10.9 0.6 %copy.13 = bf16[16,16,128]{2,1,0:T(8,128)(2,1)} copy(bf16[16,16,128]{2,1,0:T(8,128)(2,1)S(1)} %shard_map.109) | data formatting | bytes 131072

commit v6 on v5

--- a/solution.py
+++ b/solution.py
@@ -69,9 +69,7 @@
 def kernel(
     sizes,
     near_list_in,
-    near_mask_in,
     far_list_in,
-    far_mask_in,
     vectors,
     basis,
     near_blocks,
@@ -81,9 +79,7 @@
     coupling_top,
     out,
     near_list,
-    near_mask,
     far_list,
-    far_mask,
     vec_buf,
     basis_buf,
     near_buf,
@@ -120,10 +116,8 @@
         (basis, basis_buf),
         (transfer_low, tlow_buf),
         (near_list_in, near_list),
-        (near_mask_in, near_mask),
         (near_blocks, near_buf),
         (far_list_in, far_list),
-        (far_mask_in, far_mask),
         (coupling_low, clow_buf),
         (transfer_top, ttop_buf),
     ]
@@ -136,6 +130,7 @@
     ]
     for copy in copies[:3]:
         copy.start()
+    rim_in[:, pl.ds(0, RIM)] = jnp.zeros((2, RIM) + rim_in.shape[2:], BF16)
     lax.fori_loop(1, tree_devs, greet, 0, unroll=tree_devs <= 16)
     for copy in copies[3:]:
         copy.start()
@@ -219,7 +214,8 @@
     sources = []
     root_row = starts[low_levels - 1]
     for slot in range(k_far):
-        spot = jnp.where(far_mask[slot, root_row] != 0, far_list[slot, root_row], tree_devs)
+        spot = far_list[slot, root_row]
+        spot = jnp.where(spot == device, tree_devs, spot)
         near_path = clow_buf[root_row, slot]
         path_buf[len(sources)] = jnp.concatenate([near_path, jnp.zeros_like(near_path)], axis=-1)
         sources.append(spot)
@@ -298,13 +294,11 @@
 
     def near_step(leaf, carry):
         beside = []
-        for slot in range(k_near):
-            spot = jnp.where(
-                near_mask[slot, leaf] != 0,
-                near_list[slot, leaf] - near_base,
-                leaves + 2 * RIM,
-            )
-            beside.append(vec_buf[spot])
+        for step in (-1, 0, 1):
+            beside.append(vec_buf[RIM + leaf + step])
+        for slot in range(3, k_near):
+            spot = jnp.maximum(near_list[slot, leaf] - near_base, 0)
+            beside.append(vec_buf[jnp.where(spot == RIM + leaf, leaves + 2 * RIM, spot)])
         blocks = near_buf[leaf]
         near_acc[leaf] = dot(
             jnp.concatenate(beside, axis=-1),
@@ -323,9 +317,8 @@
             row = starts[height] + box
             total = None
             for slot in range(k_far):
-                spot = jnp.where(
-                    far_mask[slot, row] != 0, far_list[slot, row] - far_base, zero_spot
-                )
+                spot = jnp.maximum(far_list[slot, row] - far_base, 0)
+                spot = jnp.where(spot == rims[height] + box, zero_spot, spot)
                 term = dot(buf[spot], clow_buf[row, slot])
                 total = term if total is None else total + term
             far_acc[row] = folded(total)
@@ -402,8 +395,6 @@
     paths = k_far * sum(1 << height for height in range(top_used + 1))
     scratch = [
         pltpu.SMEM(near_list.shape[::-1], jnp.int32),
-        pltpu.SMEM(near_list.shape[::-1], jnp.int32),
-        pltpu.SMEM(far_list.shape[::-1], jnp.int32),
         pltpu.SMEM(far_list.shape[::-1], jnp.int32),
         pltpu.VMEM((leaves + 2 * RIM + 1, num_vectors, points), BF16),
         pltpu.VMEM(leaf_basis.shape, BF16),
@@ -420,7 +411,7 @@
         pltpu.VMEM((2, rim_boxes, num_vectors, points), BF16),
         pltpu.VMEM((paths, rank, 2 * rank), BF16),
         pltpu.VMEM((leaves, 2 * rank, points), BF16),
-        pltpu.SemaphoreType.DMA((10 + top_used,)),
+        pltpu.SemaphoreType.DMA((8 + top_used,)),
         pltpu.SemaphoreType.DMA((2,)),
         pltpu.SemaphoreType.DMA((2,)),
         pltpu.SemaphoreType.DMA,
@@ -430,7 +421,7 @@
     return pl.pallas_call(
         functools.partial(kernel, sizes),
         out_shape=pltpu.VMEM(vectors.shape, BF16),
-        in_specs=[pl.BlockSpec(memory_space=pltpu.HBM)] * 11,
+        in_specs=[pl.BlockSpec(memory_space=pltpu.HBM)] * 9,
         out_specs=pl.BlockSpec(memory_space=pltpu.VMEM),
         scratch_shapes=scratch,
         compiler_params=pltpu.CompilerParams(
@@ -438,9 +429,7 @@
         ),
     )(
         near_list.T,
-        near_mask.T,
         far_list.T,
-        far_mask.T,
         vectors,
         leaf_basis,
         near_blocks,

time: 11.7 us -> 11.7 us (level)
  no operation moved by 1% of the time
where the time goes in v6:
time: 11.7 us; the launch traced here: 11.5 us
  Pallas kernels  10.9 us (93%)
  local copies, waits for them, and re-layouts  0.63 us (5%)
    pallas_call x1, Pallas kernels, per_device(): pl.pallas_call(functools.partial(kernel, sizes), out_shape=pltpu.VMEM(vec...  10.9 us
    unnamed x1, local copies, waits for them, and re-layouts  0.63 us

profile of v6, /device:TPU:1, one launch (start us, length us, event | category | flops | bytes accessed | tf_op | source)
XLA Modules:
  0.0 11.5 jit_solution(12696342474105848641)
XLA Ops:
  0.0 10.9 %shard_map.91 = bf16[16,16,128]{2,1,0:T(8,128)(2,1)S(1)} custom-call(s32[6,16]{1,0:T(8,128)} %bitcast.2, s32[3,31]{1,0:T(4,128)} %bitcast.3, bf16[16,16,128]{2,1,0:T(8,128)(2,1)} %vectors.1, bf16[16,64,128]{2,1,0:T(8,128)(2,1)} %basis.1, bf16[16,6,128,128]{3,2,1,0:T(8,128)(2,1)} %near_blocks.1, bf16[30,64,64]{2,1,0:T(8,128)(2,1)} %transfer_low.1, ...), custom_call_target="tpu_custom_call" | custom-call | tf_op jit(solution)/shard_map/pallas_call | solution.py:421
  10.9 0.6 %copy.11 = bf16[16,16,128]{2,1,0:T(8,128)(2,1)} copy(bf16[16,16,128]{2,1,0:T(8,128)(2,1)S(1)} %shard_map.91) | data formatting | bytes 131072
